TPU v7x, 512 devices: a whole 4x8x8 slice. The times are simulated.
512 devices in a mesh: src: 32 (over z, y_hi), tgt: 16 (over y_lo, x, core).
Axes of the slice: x: 4, y: 8 (y_hi: 4, y_lo: 2; y = y_hi * 2 + y_lo), z: 8, core: 2. Of those that a mesh axis runs over, the one named last changes fastest.
Arguments:
- source_points: float32 [3, 131072], P(None, 'src'), may hold values from -3.5 to 3.5, as said below
- target_points: float32 [3, 65536], P(None, 'tgt'), may hold values from -3.5 to 3.5, as said below
- source_weight: float32 [131072], P('src'), may hold values from 0.1 to 3
- target_weight: float32 [65536], P('tgt'), may hold values from 0.1 to 3
- target_start: float32 [65536], P('tgt'), may hold values from -1.2 to 1.2
- tile_source: int32 [32, 16, 12], P('src', 'tgt'), may hold values from 0 to 7, as said below
- tile_target: int32 [32, 16, 12], P('src', 'tgt'), may hold values from 0 to 7, as said below
- tile_count: int32 [32, 16], P('src', 'tgt'), may hold values from 8 to 12, as said below
Outputs:
- source_potential: float32 [131072], P('src')
- target_potential: float32 [65536], P('tgt')
- source_gradient: float32 [3, 131072], P(None, ('src', 'tgt'))
- target_gradient: float32 [3, 65536], P(None, 'tgt')
Inputs may be any that keep to these rules, and one draw needn't show every extreme that they name: `source_points`: coordinates are cluster centres plus offsets. `target_points`: coordinates are cluster centres plus offsets. `tile_source`: within one block pair the live slots name distinct cluster pairs; the first 8 slots name every source cluster of the block once and every target cluster of the block once; slots from tile_count on hold 0. `tile_target`: as for tile_source. `tile_count`: some block pair uses all 12 slots.
All inputs are finite; a program needn't handle non-finite values.
Results may differ from a plain program's by a relative error of at most 0.0003.
Values sent between devices are 32-bit elements; how exact they have to be, the bound alone decides.
A program may use at most 64 MiB of HBM per device.

v0:
```python
import jax
import jax.numpy as jnp
from jax import lax
from jax.sharding import PartitionSpec as P

CLUSTER = 512
ITERS = 2


EPSILON = 0.02
FLOOR = -1e30


def tile_offsets(xs, ys):
    return [xs[c][:, None] - ys[c][None, :] for c in range(3)]


def tile_cost(offsets):
    return 0.5 * (offsets[0] * offsets[0] + offsets[1] * offsets[1] + offsets[2] * offsets[2])


def combine_parts(first, second):
    top = jnp.maximum(first[0], second[0])
    total = first[1] * jnp.exp(first[0] - top) + second[1] * jnp.exp(second[0] - top)
    return (top, total)


def reduce_rows(tops, totals):
    largest = lax.pmax(tops, "tgt")
    return (largest, lax.psum(totals * jnp.exp(tops - largest), "tgt"))


def reduce_cols(tops, totals):
    largest = lax.pmax(tops, "src")
    return (largest, lax.psum(totals * jnp.exp(tops - largest), "src"))


def body(
    source_points,
    target_points,
    source_weight,
    target_weight,
    target_start,
    tile_source,
    tile_target,
    tile_count,
):
    width_src = source_points.shape[1]
    width_tgt = target_points.shape[1]
    slots = tile_source.shape[2]
    pairs_src = tile_source[0, 0]
    pairs_tgt = tile_target[0, 0]
    live_count = tile_count[0, 0]
    log_source = jnp.log(source_weight)
    log_target = jnp.log(target_weight)

    def tile_points(slot):
        srow = pairs_src[slot] * CLUSTER
        tcol = pairs_tgt[slot] * CLUSTER
        xs = lax.dynamic_slice_in_dim(source_points, srow, CLUSTER, 1)
        ys = lax.dynamic_slice_in_dim(target_points, tcol, CLUSTER, 1)
        return (srow, tcol, tile_offsets(xs, ys))

    def run_tiles(step, init):
        return lax.fori_loop(0, slots, step, init)

    def row_pass(target_pot):

        def step(slot, carry):
            tops, totals = carry
            srow, tcol, offs = tile_points(slot)
            lb = lax.dynamic_slice_in_dim(log_target, tcol, CLUSTER)
            gs = lax.dynamic_slice_in_dim(target_pot, tcol, CLUSTER)
            scores = lb[None, :] + (gs[None, :] - tile_cost(offs)) / EPSILON
            part_top = jnp.max(scores, axis=1)
            part_total = jnp.sum(jnp.exp(scores - part_top[:, None]), axis=1)
            live = slot < live_count
            part_top = jnp.where(live, part_top, FLOOR)
            part_total = jnp.where(live, part_total, 0.0)
            old = (
                lax.dynamic_slice_in_dim(tops, srow, CLUSTER),
                lax.dynamic_slice_in_dim(totals, srow, CLUSTER),
            )
            new = combine_parts(old, (part_top, part_total))
            tops = lax.dynamic_update_slice_in_dim(tops, new[0], srow, 0)
            totals = lax.dynamic_update_slice_in_dim(totals, new[1], srow, 0)
            return (tops, totals)

        init = (jnp.full((width_src,), FLOOR, jnp.float32), jnp.zeros((width_src,), jnp.float32))
        tops, totals = run_tiles(step, init)
        tops, totals = reduce_rows(tops, totals)
        return -EPSILON * (tops + jnp.log(totals))

    def col_pass(source_pot):

        def step(slot, carry):
            tops, totals = carry
            srow, tcol, offs = tile_points(slot)
            la = lax.dynamic_slice_in_dim(log_source, srow, CLUSTER)
            fs = lax.dynamic_slice_in_dim(source_pot, srow, CLUSTER)
            scores = la[:, None] + (fs[:, None] - tile_cost(offs)) / EPSILON
            part_top = jnp.max(scores, axis=0)
            part_total = jnp.sum(jnp.exp(scores - part_top[None, :]), axis=0)
            live = slot < live_count
            part_top = jnp.where(live, part_top, FLOOR)
            part_total = jnp.where(live, part_total, 0.0)
            old = (
                lax.dynamic_slice_in_dim(tops, tcol, CLUSTER),
                lax.dynamic_slice_in_dim(totals, tcol, CLUSTER),
            )
            new = combine_parts(old, (part_top, part_total))
            tops = lax.dynamic_update_slice_in_dim(tops, new[0], tcol, 0)
            totals = lax.dynamic_update_slice_in_dim(totals, new[1], tcol, 0)
            return (tops, totals)

        init = (jnp.full((width_tgt,), FLOOR, jnp.float32), jnp.zeros((width_tgt,), jnp.float32))
        tops, totals = run_tiles(step, init)
        tops, totals = reduce_cols(tops, totals)
        return -EPSILON * (tops + jnp.log(totals))

    target_pot = target_start
    source_pot = source_weight
    for turn in range(ITERS):
        source_pot = row_pass(target_pot)
        target_pot = col_pass(source_pot)

    def grad_step(slot, carry):
        grad_src, grad_tgt = carry
        srow, tcol, offs = tile_points(slot)
        la = lax.dynamic_slice_in_dim(log_source, srow, CLUSTER)
        lb = lax.dynamic_slice_in_dim(log_target, tcol, CLUSTER)
        fs = lax.dynamic_slice_in_dim(source_pot, srow, CLUSTER)
        gs = lax.dynamic_slice_in_dim(target_pot, tcol, CLUSTER)
        plan = jnp.exp(
            la[:, None] + lb[None, :] + (fs[:, None] + gs[None, :] - tile_cost(offs)) / EPSILON
        )
        plan = jnp.where(slot < live_count, plan, 0.0)
        src_part = jnp.stack([jnp.sum(plan * offs[c], axis=1) for c in range(3)])
        tgt_part = jnp.stack([-jnp.sum(plan * offs[c], axis=0) for c in range(3)])
        grad_src = lax.dynamic_update_slice_in_dim(
            grad_src, lax.dynamic_slice_in_dim(grad_src, srow, CLUSTER, 1) + src_part, srow, 1
        )
        grad_tgt = lax.dynamic_update_slice_in_dim(
            grad_tgt, lax.dynamic_slice_in_dim(grad_tgt, tcol, CLUSTER, 1) + tgt_part, tcol, 1
        )
        return (grad_src, grad_tgt)

    init = (jnp.zeros((3, width_src), jnp.float32), jnp.zeros((3, width_tgt), jnp.float32))
    grad_src, grad_tgt = run_tiles(grad_step, init)
    whole_grad = lax.psum(grad_src, "tgt")
    share = width_src // lax.axis_size("tgt")
    own_grad = lax.dynamic_slice_in_dim(whole_grad, lax.axis_index("tgt") * share, share, 1)
    target_grad = lax.psum(grad_tgt, "src")
    return (source_pot, target_pot, own_grad, target_grad)


def solution(mesh):
    return jax.shard_map(
        body,
        mesh=mesh,
        in_specs=(
            P(None, "src"),
            P(None, "tgt"),
            P("src"),
            P("tgt"),
            P("tgt"),
            P("src", "tgt", None),
            P("src", "tgt", None),
            P("src", "tgt"),
        ),
        out_specs=(P("src"), P("tgt"), P(None, ("src", "tgt")), P(None, "tgt")),
        check_vma=False,
    )
```

profile of v0, /device:TPU:6, one launch (start us, length us, event | category | flops | bytes accessed | tf_op | source)
XLA Modules:
  0.0 1402.8 jit_solution(12051076495140641393)
XLA Ops:
  2.0 78.2 %while.75 = (s32[]{:T(128)}, f32[4096]{0:T(1024)S(1)}, f32[4096]{0:T(1024)S(1)}, s32[12]{0:T(128)S(1)}, s32[]{:T(128)}, /*index=5*/s32[12]{0:T(128)S(1)}, f32[40...) while((s32[]{:T(128)}, f32[4096]{0:T(1024)S(1)}, ...), condition=%wide.region_3.4_spmd, body=%wide.region_0.3_spmd.sunk | while | flops 7080973 | bytes 84295 | solution.py:65
  50.1 1.0 constant_dynamic-slice_fusion.15
  69.7 1.0 constant_dynamic-slice_fusion.15
  80.3 49.9 %pmax.28 = f32[4096]{0:T(1024)S(1)} all-reduce(f32[4096]{0:T(1024)S(1)} %get-tuple-element.884), channel_id=1, replica_groups=mesh['src'=32,'tgt'=16] {'tgt'}, use_global_device_ids=true, to_apply=%region_4.5 | all-reduce | flops 4096 | bytes 32768 | tf_op jit(solution)/shard_map/pmax | solution.py:29
  130.2 52.9 %psum.42 = f32[4096]{0:T(1024)S(1)} all-reduce(f32[4096]{0:T(1024)S(1)} %exponential_multiply_fusion.3), channel_id=1, replica_groups=mesh['src'=32,'tgt'=16] {'tgt'}, use_global_device_ids=true, to_apply=%region_5.6 | all-reduce | flops 4096 | bytes 32768 | tf_op jit(solution)/shard_map/psum | solution.py:30
  183.9 68.0 %while.76 = (s32[]{:T(128)}, f32[4096]{0:T(1024)S(1)}, f32[4096]{0:T(1024)S(1)}, s32[12]{0:T(128)S(1)}, s32[]{:T(128)}, /*index=5*/s32[12]{0:T(128)S(1)}, f32[40...) while((s32[]{:T(128)}, f32[4096]{0:T(1024)S(1)}, ...), condition=%wide.region_9.10_spmd, body=%wide.region_6.9_spmd.sunk | while | flops 7080973 | bytes 84295 | solution.py:65
  226.0 1.0 constant_dynamic-slice_fusion.16
  251.9 164.7 %pmax.29 = f32[4096]{0:T(1024)S(1)} all-reduce(f32[4096]{0:T(1024)S(1)} %get-tuple-element.886), channel_id=1, replica_groups=mesh['src'=32,'tgt'=16] {'src'}, use_global_device_ids=true, to_apply=%region_10.11 | all-reduce | flops 4096 | bytes 32768 | tf_op jit(solution)/shard_map/pmax | solution.py:34
  416.6 152.1 %psum.43 = f32[4096]{0:T(1024)S(1)} all-reduce(f32[4096]{0:T(1024)S(1)} %exponential_multiply_fusion.2), channel_id=1, replica_groups=mesh['src'=32,'tgt'=16] {'src'}, use_global_device_ids=true, to_apply=%region_11.12 | all-reduce | flops 4096 | bytes 32768 | tf_op jit(solution)/shard_map/psum | solution.py:35
  568.7 70.0 %while.77 = (s32[]{:T(128)}, f32[4096]{0:T(1024)S(1)}, f32[4096]{0:T(1024)S(1)}, s32[12]{0:T(128)S(1)}, s32[]{:T(128)}, /*index=5*/s32[12]{0:T(128)S(1)}, f32[40...) while((s32[]{:T(128)}, f32[4096]{0:T(1024)S(1)}, ...), condition=%wide.region_15.16_spmd, body=%wide.region_12.15_spmd.sunk | while | flops 7080973 | bytes 84295 | solution.py:65
  612.1 1.0 constant_dynamic-slice_fusion.17
  638.7 53.1 %pmax.30 = f32[4096]{0:T(1024)S(1)} all-reduce(f32[4096]{0:T(1024)S(1)} %get-tuple-element.888), channel_id=1, replica_groups=mesh['src'=32,'tgt'=16] {'tgt'}, use_global_device_ids=true, to_apply=%region_16.17 | all-reduce | flops 4096 | bytes 32768 | tf_op jit(solution)/shard_map/pmax | solution.py:29
  691.8 52.9 %psum.44 = f32[4096]{0:T(1024)S(1)} all-reduce(f32[4096]{0:T(1024)S(1)} %exponential_multiply_fusion.1), channel_id=1, replica_groups=mesh['src'=32,'tgt'=16] {'tgt'}, use_global_device_ids=true, to_apply=%region_17.18 | all-reduce | flops 4096 | bytes 32768 | tf_op jit(solution)/shard_map/psum | solution.py:30
  744.8 68.0 %while.78 = (s32[]{:T(128)}, f32[4096]{0:T(1024)S(1)}, f32[4096]{0:T(1024)S(1)}, s32[12]{0:T(128)S(1)}, s32[]{:T(128)}, /*index=5*/s32[12]{0:T(128)S(1)}, f32[40...) while((s32[]{:T(128)}, f32[4096]{0:T(1024)S(1)}, ...), condition=%wide.region_21.22_spmd, body=%wide.region_18.21_spmd.sunk | while | flops 7080973 | bytes 84295 | solution.py:65
  786.9 1.0 constant_dynamic-slice_fusion.18
  812.8 152.1 %pmax.31 = f32[4096]{0:T(1024)S(1)} all-reduce(f32[4096]{0:T(1024)S(1)} %get-tuple-element.890), channel_id=1, replica_groups=mesh['src'=32,'tgt'=16] {'src'}, use_global_device_ids=true, to_apply=%region_22.23 | all-reduce | flops 4096 | bytes 32768 | tf_op jit(solution)/shard_map/pmax | solution.py:34
  964.9 152.1 %psum.45 = f32[4096]{0:T(1024)S(1)} all-reduce(f32[4096]{0:T(1024)S(1)} %exponential_multiply_fusion), channel_id=1, replica_groups=mesh['src'=32,'tgt'=16] {'src'}, use_global_device_ids=true, to_apply=%region_23.24 | all-reduce | flops 4096 | bytes 32768 | tf_op jit(solution)/shard_map/psum | solution.py:35
  1117.0 79.6 %while.79 = (s32[]{:T(128)}, f32[3,4096]{1,0:T(4,128)S(1)}, f32[3,4096]{1,0:T(4,128)S(1)}, s32[12]{0:T(128)S(1)}, s32[]{:T(128)}, /*index=5*/f32[4096]{0:T(1024)...) while((s32[]{:T(128)}, f32[3,4096]{1,0:T(4,128)S(1)}, ...), condition=%wide.region_31.32_spmd, body=%wide.region_24.31_spmd.sunk | while | flops 6299149 | bytes 131435 | solution.py:65
  1122.2 1.3 fusion.36
  1128.8 1.3 fusion.36
  1135.5 1.3 fusion.36
  1142.1 1.3 fusion.36
  1148.8 1.3 fusion.36
  1155.4 1.3 fusion.36
  1162.0 1.3 fusion.36
  1168.7 1.3 fusion.36
  1175.3 1.3 fusion.36
  1181.9 1.3 fusion.36
  1188.6 1.3 fusion.36
  1195.2 1.3 fusion.36
  1196.6 52.9 %psum.46 = f32[3,4096]{1,0:T(4,128)S(1)} all-reduce(f32[3,4096]{1,0:T(4,128)S(1)} %get-tuple-element.892), channel_id=1, replica_groups=mesh['src'=32,'tgt'=16] {'tgt'}, use_global_device_ids=true, to_apply=%region_32.33 | all-reduce | flops 12288 | bytes 98304 | tf_op jit(solution)/shard_map/psum | solution.py:150
  1250.2 152.6 %psum.47 = f32[3,4096]{1,0:T(4,128)} all-reduce(f32[3,4096]{1,0:T(4,128)S(1)} %get-tuple-element.893), channel_id=1, replica_groups=mesh['src'=32,'tgt'=16] {'src'}, use_global_device_ids=true, to_apply=%region_33.34 | all-reduce | flops 12288 | bytes 98304 | tf_op jit(solution)/shard_map/psum | solution.py:153
  (554 shorter events, 226.0 us)
Async XLA Ops:
  1.4 0.7 copy-start.3
  1.4 0.7 copy-start.4
  183.1 0.7 copy-start.2
  1196.6 52.9 %copy-start = (f32[4096]{0:T(1024)}, f32[4096]{0:T(1024)S(1)}, u32[]{:S(2)}) copy-start(f32[4096]{0:T(1024)S(1)} %get-tuple-element.1724) | copy-start | bytes 49156
  1196.6 52.9 %copy-start.1 = (f32[4096]{0:T(1024)}, f32[4096]{0:T(1024)S(1)}, u32[]{:S(2)}) copy-start(f32[4096]{0:T(1024)S(1)} %get-tuple-element.1725) | copy-start | bytes 49156
where the time goes:
time: 1420 us; the launch traced here: 1400 us
  blocking collectives  1040 us (73%)
  local copies, waits for them, and re-layouts  158 us (11%)
  loops' own time  120 us (8%)
  other arithmetic  89 us (6%)
    pmax x2, blocking collectives, reduce_cols(): largest = lax.pmax(tops, 'src')  317 us
    psum x2, blocking collectives, reduce_cols(): return (largest, lax.psum(totals * jnp.exp(tops - largest), 'src'))  304 us
    psum x1, blocking collectives, body(): target_grad = lax.psum(grad_tgt, 'src')  153 us
    another operation x5, loops' own time, run_tiles(): return lax.fori_loop(0, slots, step, init)  120 us
    psum x2, blocking collectives, reduce_rows(): return (largest, lax.psum(totals * jnp.exp(tops - largest), 'tgt'))  106 us
    pmax x2, blocking collectives, reduce_rows(): largest = lax.pmax(tops, 'tgt')  103 us
    slice x72, local copies, waits for them, and re-layouts, tile_offsets(): return [xs[c][:, None] - ys[c][None, :] for c in range(3)]  65.2 us
    psum x1, blocking collectives, body(): whole_grad = lax.psum(grad_src, 'tgt')  52.9 us

commit v1 on v0

v1 whole, which is shorter than its diff:
```python
import functools
import math

import jax
import jax.numpy as jnp
from jax import lax
from jax.experimental import pallas as pl
from jax.experimental.pallas import tpu as pltpu
from jax.sharding import PartitionSpec as P

ITERS = 2
CPD = 8
Y_HI = 4
EPSILON = 0.02
FLOOR = -1e30
R = math.sqrt(math.log2(math.e) / EPSILON)
BACK = EPSILON * math.log(2.0)
MESH = pl.DeviceIdType.MESH
F32 = jnp.float32
BF16 = jnp.bfloat16


def split3(v):
    one = v.astype(BF16).astype(F32)
    rest = v - one
    two = rest.astype(BF16).astype(F32)
    return one, two, rest - two


def logsum(parts):
    top = functools.reduce(jnp.maximum, parts)
    return top + jnp.log2(functools.reduce(jnp.add, [jnp.exp2(p - top) for p in parts]))


def kernel(n_src, n_tgt, slots, C, x_ref, y_ref, a_ref, b_ref, g_ref, ts_ref, tt_ref, tc_ref,
           f_out, g_out, sg_out, tg_out,
           xs, ys, xt, yt, cl, bias, tops, sums, ehi, elo, tx, gs,
           rbuf, ybuf, zbuf, xbar, xybuf, xzbuf, xtbuf, dsend, dbuf, ssem, rsem):
    n_z = n_src // Y_HI
    s = lax.axis_index("src")
    t = lax.axis_index("tgt")
    z = s // Y_HI
    h = lax.rem(s, Y_HI)
    tgt_peers = [(s, lax.rem(t + k, n_tgt)) for k in range(1, n_tgt)]
    y_peers = [(z * Y_HI + lax.rem(h + k, Y_HI), t) for k in range(1, Y_HI)]
    z_peers = [(lax.rem(z + k, n_z) * Y_HI + h, t) for k in range(1, n_z)]
    everyone = tgt_peers + y_peers + z_peers

    barrier = pltpu.get_barrier_semaphore()
    for peer in everyone:
        pl.semaphore_signal(barrier, inc=1, device_id=peer, device_id_type=MESH)

    def send(no, src, dst, peer):
        pltpu.make_async_remote_copy(src_ref=src, dst_ref=dst, send_sem=ssem.at[no], recv_sem=rsem.at[no],
                                     device_id=peer, device_id_type=MESH).start()

    def waiter(no, like):
        return pltpu.make_async_remote_copy(src_ref=like, dst_ref=like, send_sem=ssem.at[no], recv_sem=rsem.at[no],
                                            device_id=everyone[0], device_id_type=MESH)

    row8 = lax.broadcasted_iota(jnp.int32, (8, C), 0)
    row24 = lax.rem(lax.broadcasted_iota(jnp.int32, (24, C), 0), 8)
    for c in range(CPD):
        at = pl.ds(c * C, C)
        for ref, full, stat, norm, ones in ((x_ref, xt, xs, 3, 1.0), (y_ref, yt, ys, 4, 0.0)):
            p3 = ref[:, at] * R
            full[c, 0:3, :] = p3
            full[c, 3:6, :] = p3
            full[c, 6:8, :] = jnp.ones((2, C), F32)
            v = full[c]
            coord = row8 < 6
            one, two, three = split3(jnp.where(coord, v, 0.0))
            if norm == 3:
                a = jnp.where(row8 < 3, one, two) + jnp.where(row8 == 6, 1.0, 0.0)
                stat[c] = jnp.concatenate([a, jnp.where(row8 < 3, one, two), jnp.where(row8 < 3, one, three)], 0)
            else:
                stat[c] = jnp.concatenate([one, two, jnp.where(row8 < 3, three, one)], 0)
            cl[norm, c:c + 1, :] = 0.5 * jnp.sum(jnp.where(row8 < 3, v * v, 0.0), axis=0, keepdims=True)
        cl[0, c:c + 1, :] = a_ref[:, at]
        cl[1, c:c + 1, :] = b_ref[:, at]
        cl[2, c:c + 1, :] = g_ref[:, at]
    cl[0] = jnp.log2(cl[0])
    cl[1] = jnp.log2(cl[1])
    v = cl[2] * (1.0 / BACK) - cl[4]

    count = tc_ref[0, 0]

    def owners(ref):
        return [jnp.where(k < count, ref[0, 0, k], -1) for k in range(slots)]

    def tile_scores(summed, own, summed_index, own_index):
        lhs = jnp.concatenate([summed[summed_index], bias[...]], 0).astype(BF16)
        pick = jnp.where(row24 == summed_index, 1.0, 0.0)
        rhs = jnp.concatenate([own[own_index], pick], 0).astype(BF16)
        return lax.dot_general(lhs, rhs, (((0,), (0,)), ((), ())), preferred_element_type=F32)

    def set_bias(value):
        one, two, three = split3(value)
        bias[0:8, :] = one
        bias[8:16, :] = two
        bias[16:24, :] = three

    def one_pass(value, summed, own, summed_ref, own_ref):
        set_bias(value)

        def tile(k, carry):
            scores = tile_scores(summed, own, summed_ref[0, 0, k], own_ref[0, 0, k])
            top = jnp.max(scores, axis=0, keepdims=True)
            tops[pl.ds(k, 1), :] = top
            sums[pl.ds(k, 1), :] = jnp.sum(jnp.exp2(scores - top), axis=0, keepdims=True)
            return carry
        lax.fori_loop(0, slots, tile, 0)

    def merge(own_ref):
        own = owners(own_ref)
        masks = [row8 == own[k] for k in range(slots)]
        top = jnp.full((8, C), FLOOR, F32)
        for k in range(slots):
            top = jnp.maximum(top, jnp.where(masks[k], tops[k:k + 1, :], FLOOR))
        scales = [jnp.where(masks[k], jnp.exp2(tops[k:k + 1, :] - top), 0.0) for k in range(slots)]
        total = functools.reduce(jnp.add, [scales[k] * sums[k:k + 1, :] for k in range(slots)])
        return top + jnp.log2(total), scales, total

    def over_tgt(turn, local):
        buf = rbuf.at[turn]
        buf[t] = local
        for peer in tgt_peers:
            send(turn, buf.at[t], buf.at[t], peer)
        done = waiter(turn, buf.at[pl.ds(0, n_tgt - 1)])
        done.wait_recv()
        done.wait_send()
        return -logsum([buf[k] for k in range(n_tgt)])

    def over_y(turn, local):
        buf = ybuf.at[turn]
        buf[h] = local
        for peer in y_peers:
            send(2 + turn, buf.at[h], buf.at[h], peer)

    def over_y_done(turn):
        buf = ybuf.at[turn]
        done = waiter(2 + turn, buf.at[pl.ds(0, Y_HI - 1)])
        done.wait_recv()
        done.wait_send()
        return logsum([buf[k] for k in range(Y_HI)])

    def over_z(turn, local):
        buf = zbuf.at[turn]
        buf[z] = local
        for peer in z_peers:
            send(4 + turn, buf.at[z], buf.at[z], peer)

    def over_z_done(turn):
        buf = zbuf.at[turn]
        if n_z > 1:
            done = waiter(4 + turn, buf.at[pl.ds(0, n_z - 1)])
            done.wait_recv()
            done.wait_send()
        return logsum([buf[k] for k in range(n_z)])

    one_pass(cl[1] + v, ys, xs, tt_ref, ts_ref)
    local = merge(ts_ref)[0]
    pl.semaphore_wait(barrier, len(everyone))
    u = over_tgt(0, local)
    one_pass(cl[0] + u, xs, ys, ts_ref, tt_ref)
    over_y(0, merge(tt_ref)[0])
    over_z(0, over_y_done(0))
    v = -over_z_done(0)

    one_pass(cl[1] + v, ys, xs, tt_ref, ts_ref)
    u = over_tgt(1, merge(ts_ref)[0])

    set_bias(cl[0] + u)

    def last_tile(k, carry):
        p = ts_ref[0, 0, k]
        scores = tile_scores(xs, ys, p, tt_ref[0, 0, k])
        top = jnp.max(scores, axis=0, keepdims=True)
        tops[pl.ds(k, 1), :] = top
        e = jnp.exp2(scores - top)
        big = e.astype(BF16)
        small = (e - big.astype(F32)).astype(BF16)
        ehi[k] = big
        elo[k] = small
        lhs = xs[p].astype(BF16)
        out = jnp.dot(lhs, big, preferred_element_type=F32) + jnp.dot(lhs, small, preferred_element_type=F32)
        tx[k] = out
        sums[pl.ds(k, 1), :] = out[6:7, :]
        return carry
    lax.fori_loop(0, slots, last_tile, 0)

    local, scales, total = merge(tt_ref)
    over_y(1, local)
    per = 1.0 / total
    for c in range(3):
        acc = jnp.zeros((8, C), F32)
        for k in range(slots):
            rows = tx[k, c:c + 1, :] + tx[k, 3 + c:4 + c, :] + tx[k, 19 + c:20 + c, :]
            acc = acc + scales[k] * rows
        xbar[8 * c:8 * c + 8, :] = acc * per
    W = C // Y_HI

    def lanes(who):
        return pl.ds(pl.multiple_of(who * W, W), W)

    xybuf[h] = xbar[:, lanes(h)]
    for k in range(1, Y_HI):
        who = lax.rem(h + k, Y_HI)
        send(6, xbar.at[:, lanes(who)], xybuf.at[h], y_peers[k - 1])
    f_all = (u + cl[3]) * BACK
    for c in range(CPD):
        f_out[:, c * C:(c + 1) * C] = f_all[c:c + 1, :]
    both = over_y_done(1)
    over_z(1, both)
    done = waiter(6, xybuf.at[pl.ds(0, Y_HI - 1)])
    done.wait_recv()
    done.wait_send()

    def weighted(buf, weight_buf, n, total_block):
        acc = jnp.zeros((24, W), F32)
        for k in range(n):
            part = jnp.exp2(weight_buf[k, :, lanes(h)] - total_block)
            acc = acc + buf[k] * jnp.concatenate([part, part, part], 0)
        return acc

    xzbuf[z] = weighted(xybuf, ybuf.at[1], Y_HI, zbuf[1, z, :, lanes(h)])
    for peer in z_peers:
        send(7, xzbuf.at[z], xzbuf.at[z], peer)
    v = -over_z_done(1)

    cl[2] = v
    wlog = cl[1] + v
    bias[0:8, :] = wlog

    def grad_tile(k, carry):
        q = tt_ref[0, 0, k]
        w = jnp.exp2(bias[pl.ds(q, 1), :] + tops[pl.ds(k, 1), :])
        one, two, three = split3(yt[q] * w)
        lhs = jnp.concatenate([one, two, three], 0).astype(BF16)
        dims = (((1,), (1,)), ((), ()))
        out = (lax.dot_general(lhs, ehi[k], dims, preferred_element_type=F32)
               + lax.dot_general(lhs, elo[k], dims, preferred_element_type=F32))
        gs[k] = out[0:8, :] + out[8:16, :] + out[16:24, :]
        return carry
    lax.fori_loop(0, slots, grad_tile, 0)

    own = owners(ts_ref)
    share = CPD * C // n_tgt
    per_cluster = C // share
    for c in range(CPD):
        acc = jnp.zeros((8, C), F32)
        for k in range(slots):
            acc = acc + jnp.where(own[k] == c, gs[k], 0.0)
        diff = (xt[c] * acc[6:7, :] - acc) * (1.0 / R)
        for part in range(per_cluster):
            dsend[c * per_cluster + part] = diff[0:4, part * share:(part + 1) * share]
    dbuf[t] = dsend[t]
    for k in range(1, n_tgt):
        send(8, dsend.at[lax.rem(t + k, n_tgt)], dbuf.at[t], tgt_peers[k - 1])

    if n_z > 1:
        done = waiter(7, xzbuf.at[pl.ds(0, n_z - 1)])
        done.wait_recv()
        done.wait_send()
    xtbuf[h] = weighted(xzbuf, zbuf.at[1], n_z, -cl[2, :, lanes(h)])
    for peer in y_peers:
        send(9, xtbuf.at[h], xtbuf.at[h], peer)
    g_all = (cl[2] + cl[4]) * BACK
    for c in range(CPD):
        g_out[:, c * C:(c + 1) * C] = g_all[c:c + 1, :]

    done = waiter(8, dbuf.at[pl.ds(0, n_tgt - 1)])
    done.wait_recv()
    done.wait_send()
    grad = functools.reduce(jnp.add, [dbuf[k] for k in range(n_tgt)])
    sg_out[...] = grad[0:3, :]

    done = waiter(9, xtbuf.at[pl.ds(0, Y_HI - 1)])
    done.wait_recv()
    done.wait_send()
    for k in range(Y_HI):
        block = xtbuf[k] * (1.0 / R)
        for q in range(CPD):
            at = pl.ds(q * C + k * W, W)
            mean = jnp.concatenate([block[8 * c + q:8 * c + q + 1, :] for c in range(3)], 0)
            tg_out[:, at] = b_ref[:, at] * (y_ref[:, at] - mean)


def body(x, y, a, b, g, ts, tt, tc):
    n_src = lax.axis_size("src")
    n_tgt = lax.axis_size("tgt")
    slots = ts.shape[2]
    width = x.shape[1]
    C = width // CPD
    share = width // n_tgt
    n_z = n_src // Y_HI
    vmem = pl.BlockSpec(memory_space=pltpu.VMEM)
    smem = pl.BlockSpec(memory_space=pltpu.SMEM)
    V = pltpu.VMEM
    f, g1, sg, tg = pl.pallas_call(
        functools.partial(kernel, n_src, n_tgt, slots, C),
        out_shape=(jax.ShapeDtypeStruct((1, width), F32), jax.ShapeDtypeStruct((1, width), F32),
                   jax.ShapeDtypeStruct((3, share), F32), jax.ShapeDtypeStruct((3, width), F32)),
        in_specs=[vmem] * 5 + [smem] * 3,
        out_specs=(vmem,) * 4,
        scratch_shapes=[
            V((CPD, 24, C), F32), V((CPD, 24, C), F32), V((CPD, 8, C), F32), V((CPD, 8, C), F32),
            V((5, 8, C), F32), V((24, C), F32), V((16, C), F32), V((16, C), F32),
            V((slots, C, C), BF16), V((slots, C, C), BF16), V((slots, 24, C), F32), V((slots, 8, C), F32),
            V((ITERS, n_tgt, 8, C), F32), V((ITERS, Y_HI, 8, C), F32), V((ITERS, n_z, 8, C), F32),
            V((24, C), F32), V((Y_HI, 24, C // Y_HI), F32), V((n_z, 24, C // Y_HI), F32),
            V((Y_HI, 24, C // Y_HI), F32), V((n_tgt, 4, share), F32), V((n_tgt, 4, share), F32),
            pltpu.SemaphoreType.DMA((10,)), pltpu.SemaphoreType.DMA((10,)),
        ],
        compiler_params=pltpu.CompilerParams(collective_id=0, has_side_effects=True,
                                             vmem_limit_bytes=40 * 1024 * 1024),
        name="sinkhorn",
    )(x, y, a.reshape(1, -1), b.reshape(1, -1), g.reshape(1, -1), ts, tt, tc)
    return f.reshape(-1), g1.reshape(-1), sg, tg


def solution(mesh):
    return jax.shard_map(
        body,
        mesh=mesh,
        in_specs=(P(None, "src"), P(None, "tgt"), P("src"), P("tgt"), P("tgt"),
                  P("src", "tgt", None), P("src", "tgt", None), P("src", "tgt")),
        out_specs=(P("src"), P("tgt"), P(None, ("src", "tgt")), P(None, "tgt")),
        check_vma=False,
    )
```

time: 1420 us -> 90.2 us (0.06); the launches traced: 1400 us -> 89.6 us
  blocking collectives: 1040 us -> 0 us
  local copies, waits for them, and re-layouts: 158 us -> 6.92 us
  loops' own time: 120 us -> 0 us
  other arithmetic: 89 us -> 0 us
  Pallas kernels: 0 us -> 81.4 us
    psum x6 -> x0, blocking collectives: 616 us -> none  [the longest x2 304 us: reduce_cols(): return (largest, lax.psum(totals * jnp.exp(tops - largest), 'src'))]
    pmax x4 -> x0, blocking collectives: 420 us -> none  [the longest x2 317 us: reduce_cols(): largest = lax.pmax(tops, 'src')]
    another operation x5 -> x0, loops' own time: 120 us -> none  [run_tiles(): return lax.fori_loop(0, slots, step, init)]
    dynamic_slice x265 -> x0, local copies, waits for them, and re-layouts: 90.3 us -> none  [the longest x60 35.3 us: tile_points(): tcol = pairs_tgt[slot] * CLUSTER]
    pallas_call x0 -> x1, Pallas kernels: none -> 81.4 us  [body(): pl.pallas_call(functools.partial(kernel, n_src, n_tgt, slots, C), out_sha...]
    slice x72 -> x0, local copies, waits for them, and re-layouts: 65.2 us -> none  [tile_offsets(): return [xs[c][:, None] - ys[c][None, :] for c in range(3)]]
    reduce_sum x60 -> x0, other arithmetic: 48.9 us -> none  [the longest x24 17.1 us: step(): part_total = jnp.sum(jnp.exp(scores - part_top[:, None]), axis=1)]
    reduce_max x48 -> x0, other arithmetic: 28.4 us -> none  [the longest x24 15.7 us: step(): part_top = jnp.max(scores, axis=1)]
where the time goes in v1:
time: 90.2 us; the launch traced here: 89.6 us
  Pallas kernels  81.4 us (90%)
  local copies, waits for them, and re-layouts  6.92 us (8%)
  between operations  1.31 us (1%)
    pallas_call x1, Pallas kernels, body(): pl.pallas_call(functools.partial(kernel, n_src, n_tgt, slots, C), out_sha...  81.4 us
    unnamed x18, local copies, waits for them, and re-layouts  6.92 us

profile of v1, /device:TPU:6, one launch (start us, length us, event | category | flops | bytes accessed | tf_op | source)
XLA Modules:
  0.0 89.6 jit_solution(12091629189870804709)
XLA Ops:
  1.3 0.0 copy-start.5
  1.3 0.0 copy-start.6
  1.3 0.6 copy-done.5
  1.9 0.0 copy-done.6
  2.0 0.0 copy-start
  2.0 0.8 copy-done
  2.8 0.0 copy-start.1
  2.8 0.8 copy-done.1
  3.6 0.0 copy-start.2
  3.6 0.7 copy-done.2
  4.4 0.0 copy-start.3
  4.4 0.7 copy-done.3
  5.1 0.0 copy-start.4
  5.1 0.7 copy-done.4
  5.8 81.4 %sinkhorn.1 = (f32[1,4096]{1,0:T(1,128)S(1)}, f32[1,4096]{1,0:T(1,128)S(1)}, f32[3,256]{1,0:T(4,128)S(1)}, f32[3,4096]{1,0:T(4,128)S(1)}) custom-call(f32[3,4096]{1,0:T(4,128)S(1)} %copy-done, f32[3,4096]{1,0:T(4,128)S(1)} %copy-done.1, f32[1,4096]{1,0:T(1,128)S(1)} %bitcast.7, f32[1,4096]{1,0:T(1,128)S(1)} %bitcast.8, f32[1,4096]{1,0:T(1,128)S(1)} %bitcast.9, ...), custom_call_target="tpu_custom_call" | custom-call | tf_op jit(solution)/shard_map/sinkhorn/pallas_call | solution.py:300
  87.1 0.6 copy.17
  87.8 0.6 copy.18
  88.4 0.6 copy.19
  89.0 0.6 copy.20
Async XLA Ops:
  1.3 0.7 copy-start.5
  1.3 0.7 copy-start.6
  2.0 0.8 copy-start
  2.8 0.8 copy-start.1
  3.6 0.7 copy-start.2
  4.4 0.7 copy-start.3
  5.1 0.7 copy-start.4

commit v2 on v1

--- a/solution.py
+++ b/solution.py
@@ -32,18 +32,32 @@
     return top + jnp.log2(functools.reduce(jnp.add, [jnp.exp2(p - top) for p in parts]))
 
 
-def kernel(n_src, n_tgt, slots, C, x_ref, y_ref, a_ref, b_ref, g_ref, ts_ref, tt_ref, tc_ref,
-           f_out, g_out, sg_out, tg_out,
-           xs, ys, xt, yt, cl, bias, tops, sums, ehi, elo, tx, gs,
-           rbuf, ybuf, zbuf, xbar, xybuf, xzbuf, xtbuf, dsend, dbuf, ssem, rsem):
+def kernel(n_src, n_tgt, slots, C, *refs):
+    ins, refs = refs[:8], refs[8:]
+    (f_out, g_out, sg_out, tg_out), refs = refs[:4], refs[4:]
+    held, refs = refs[:8], refs[8:]
+    (xs, ys, xt, yt, cl, bias, tops, sums, held_scores, ehi, elo, tx, gs,
+     rbuf, ybuf, zbuf, xbar, xybuf, xzbuf, xtbuf, dsend, dbuf, insem, ssem, rsem) = refs
+    x_ref, y_ref, a_ref, b_ref, g_ref, ts_ref, tt_ref, tc_ref = held
+    fetches = [pltpu.make_async_copy(ins[k], held[k], insem.at[k]) for k in range(8)]
+    for fetch in fetches:
+        fetch.start()
     n_z = n_src // Y_HI
     s = lax.axis_index("src")
     t = lax.axis_index("tgt")
     z = s // Y_HI
     h = lax.rem(s, Y_HI)
-    tgt_peers = [(s, lax.rem(t + k, n_tgt)) for k in range(1, n_tgt)]
-    y_peers = [(z * Y_HI + lax.rem(h + k, Y_HI), t) for k in range(1, Y_HI)]
-    z_peers = [(lax.rem(z + k, n_z) * Y_HI + h, t) for k in range(1, n_z)]
+    n_lo = n_tgt // 8
+    t_lo, t_x, t_core = t // 8, lax.rem(t // 2, 4), lax.rem(t, 2)
+    steps = [(dy, dx, dc) for dy in range(n_lo) for dx in range(4) for dc in range(2)][1:]
+    steps.sort(key=lambda d: -(d[0] + min(d[1], 4 - d[1]) + 0.1 * d[2]))
+    tgt_at = [lax.rem(t_lo + dy, n_lo) * 8 + lax.rem(t_x + dx, 4) * 2 + lax.rem(t_core + dc, 2)
+              for dy, dx, dc in steps]
+    tgt_peers = [(s, at) for at in tgt_at]
+    y_at = [lax.rem(h + k, Y_HI) for k in (2, 1, 3)]
+    y_peers = [(z * Y_HI + at, t) for at in y_at]
+    z_peers = [(lax.rem(z + k, n_z) * Y_HI + h, t)
+               for k in sorted(range(1, n_z), key=lambda k: -min(k, n_z - k))]
     everyone = tgt_peers + y_peers + z_peers
 
     barrier = pltpu.get_barrier_semaphore()
@@ -58,6 +72,8 @@
         return pltpu.make_async_remote_copy(src_ref=like, dst_ref=like, send_sem=ssem.at[no], recv_sem=rsem.at[no],
                                             device_id=everyone[0], device_id_type=MESH)
 
+    for fetch in fetches:
+        fetch.wait()
     row8 = lax.broadcasted_iota(jnp.int32, (8, C), 0)
     row24 = lax.rem(lax.broadcasted_iota(jnp.int32, (24, C), 0), 8)
     for c in range(CPD):
@@ -103,13 +119,19 @@
     def one_pass(value, summed, own, summed_ref, own_ref):
         set_bias(value)
 
-        def tile(k, carry):
+        def scores_of(k):
             scores = tile_scores(summed, own, summed_ref[0, 0, k], own_ref[0, 0, k])
-            top = jnp.max(scores, axis=0, keepdims=True)
+            held_scores[...] = scores
+            return jnp.max(scores, axis=0, keepdims=True)
+
+        def tile(k, top):
+            acc = jnp.exp2(held_scores[0:16, :] - top)
+            for i in range(16, C, 16):
+                acc = acc + jnp.exp2(held_scores[i:i + 16, :] - top)
             tops[pl.ds(k, 1), :] = top
-            sums[pl.ds(k, 1), :] = jnp.sum(jnp.exp2(scores - top), axis=0, keepdims=True)
-            return carry
-        lax.fori_loop(0, slots, tile, 0)
+            sums[pl.ds(k, 1), :] = jnp.sum(acc, axis=0, keepdims=True)
+            return scores_of(jnp.minimum(k + 1, slots - 1))
+        lax.fori_loop(0, slots, tile, scores_of(0), unroll=4)
 
     def merge(own_ref):
         own = owners(own_ref)
@@ -170,28 +192,26 @@
     one_pass(cl[1] + v, ys, xs, tt_ref, ts_ref)
     u = over_tgt(1, merge(ts_ref)[0])
 
-    set_bias(cl[0] + u)
-
-    def last_tile(k, carry):
+    one_pass(cl[0] + u, xs, ys, ts_ref, tt_ref)
+    local, scales, _ = merge(tt_ref)
+    over_y(1, local)
+
+    def mean_tile(k, carry):
         p = ts_ref[0, 0, k]
-        scores = tile_scores(xs, ys, p, tt_ref[0, 0, k])
-        top = jnp.max(scores, axis=0, keepdims=True)
-        tops[pl.ds(k, 1), :] = top
-        e = jnp.exp2(scores - top)
+        e = jnp.exp2(tile_scores(xs, ys, p, tt_ref[0, 0, k]) - tops[pl.ds(k, 1), :])
         big = e.astype(BF16)
         small = (e - big.astype(F32)).astype(BF16)
-        ehi[k] = big
-        elo[k] = small
         lhs = xs[p].astype(BF16)
-        out = jnp.dot(lhs, big, preferred_element_type=F32) + jnp.dot(lhs, small, preferred_element_type=F32)
-        tx[k] = out
-        sums[pl.ds(k, 1), :] = out[6:7, :]
+        tx[k] = jnp.dot(lhs, big, preferred_element_type=F32) + jnp.dot(lhs, small, preferred_element_type=F32)
         return carry
-    lax.fori_loop(0, slots, last_tile, 0)
-
-    local, scales, total = merge(tt_ref)
-    over_y(1, local)
-    per = 1.0 / total
+
+    first = max(slots - 4, 0) // 4 * 4
+    lax.fori_loop(0, first, mean_tile, 0, unroll=4)
+    both = over_y_done(1)
+    over_z(1, both)
+    lax.fori_loop(first, slots, mean_tile, 0, unroll=4)
+
+    per = 1.0 / functools.reduce(jnp.add, [scales[k] * tx[k, 6:7, :] for k in range(slots)])
     for c in range(3):
         acc = jnp.zeros((8, C), F32)
         for k in range(slots):
@@ -204,14 +224,28 @@
         return pl.ds(pl.multiple_of(who * W, W), W)
 
     xybuf[h] = xbar[:, lanes(h)]
-    for k in range(1, Y_HI):
-        who = lax.rem(h + k, Y_HI)
-        send(6, xbar.at[:, lanes(who)], xybuf.at[h], y_peers[k - 1])
+    for at, peer in zip(y_at, y_peers):
+        send(6, xbar.at[:, lanes(at)], xybuf.at[h], peer)
+
+    row8_one = jnp.where(row8 < 3, 1.0, 0.0)
+    blank = jnp.zeros((8, C), F32)
+
+    def plan_tile(k, carry):
+        p = ts_ref[0, 0, k]
+        one, two, three = split3(-tops[pl.ds(k, 1), :])
+        shift = jnp.where(row8 == 0, one, jnp.where(row8 == 1, two, jnp.where(row8 == 2, three, 0.0)))
+        pick = jnp.where(row24 == p, 1.0, 0.0)
+        lhs = jnp.concatenate([ys[tt_ref[0, 0, k]], pick, shift, blank], 0).astype(BF16)
+        rhs = jnp.concatenate([xs[p], bias[...], row8_one, blank], 0).astype(BF16)
+        e = jnp.exp2(lax.dot_general(lhs, rhs, (((0,), (0,)), ((), ())), preferred_element_type=F32))
+        big = e.astype(BF16)
+        ehi[k] = big
+        elo[k] = (e - big.astype(F32)).astype(BF16)
+        return carry
+    lax.fori_loop(0, slots, plan_tile, 0, unroll=4)
     f_all = (u + cl[3]) * BACK
     for c in range(CPD):
         f_out[:, c * C:(c + 1) * C] = f_all[c:c + 1, :]
-    both = over_y_done(1)
-    over_z(1, both)
     done = waiter(6, xybuf.at[pl.ds(0, Y_HI - 1)])
     done.wait_recv()
     done.wait_send()
@@ -237,12 +271,11 @@
         w = jnp.exp2(bias[pl.ds(q, 1), :] + tops[pl.ds(k, 1), :])
         one, two, three = split3(yt[q] * w)
         lhs = jnp.concatenate([one, two, three], 0).astype(BF16)
-        dims = (((1,), (1,)), ((), ()))
-        out = (lax.dot_general(lhs, ehi[k], dims, preferred_element_type=F32)
-               + lax.dot_general(lhs, elo[k], dims, preferred_element_type=F32))
+        out = (jnp.dot(lhs, ehi[k], preferred_element_type=F32)
+               + jnp.dot(lhs, elo[k], preferred_element_type=F32))
         gs[k] = out[0:8, :] + out[8:16, :] + out[16:24, :]
         return carry
-    lax.fori_loop(0, slots, grad_tile, 0)
+    lax.fori_loop(0, slots, grad_tile, 0, unroll=4)
 
     own = owners(ts_ref)
     share = CPD * C // n_tgt
@@ -255,8 +288,8 @@
         for part in range(per_cluster):
             dsend[c * per_cluster + part] = diff[0:4, part * share:(part + 1) * share]
     dbuf[t] = dsend[t]
-    for k in range(1, n_tgt):
-        send(8, dsend.at[lax.rem(t + k, n_tgt)], dbuf.at[t], tgt_peers[k - 1])
+    for at, peer in zip(tgt_at, tgt_peers):
+        send(8, dsend.at[at], dbuf.at[t], peer)
 
     if n_z > 1:
         done = waiter(7, xzbuf.at[pl.ds(0, n_z - 1)])
@@ -286,6 +319,29 @@
             tg_out[:, at] = b_ref[:, at] * (y_ref[:, at] - mean)
 
 
+def copy_kernel(*refs):
+    n = len(refs) // 2
+    sem = refs[-1]
+    copies = [pltpu.make_async_copy(refs[k], refs[n + k], sem.at[k]) for k in range(n)]
+    for copy in copies:
+        copy.start()
+    for copy in copies:
+        copy.wait()
+
+
+def hand_out(*arrays):
+    n = len(arrays)
+    return pl.pallas_call(
+        copy_kernel,
+        out_shape=tuple(jax.ShapeDtypeStruct(a.shape, a.dtype) for a in arrays),
+        in_specs=[pl.BlockSpec(memory_space=pltpu.HBM)] * n,
+        out_specs=(pl.BlockSpec(memory_space=pltpu.HBM),) * n,
+        scratch_shapes=[pltpu.SemaphoreType.DMA((n,))],
+        compiler_params=pltpu.CompilerParams(vmem_limit_bytes=56 * 1024 * 1024),
+        name="hand_out",
+    )(*arrays)
+
+
 def body(x, y, a, b, g, ts, tt, tc):
     n_src = lax.axis_size("src")
     n_tgt = lax.axis_size("tgt")
@@ -295,27 +351,30 @@
     share = width // n_tgt
     n_z = n_src // Y_HI
     vmem = pl.BlockSpec(memory_space=pltpu.VMEM)
-    smem = pl.BlockSpec(memory_space=pltpu.SMEM)
     V = pltpu.VMEM
     f, g1, sg, tg = pl.pallas_call(
         functools.partial(kernel, n_src, n_tgt, slots, C),
         out_shape=(jax.ShapeDtypeStruct((1, width), F32), jax.ShapeDtypeStruct((1, width), F32),
                    jax.ShapeDtypeStruct((3, share), F32), jax.ShapeDtypeStruct((3, width), F32)),
-        in_specs=[vmem] * 5 + [smem] * 3,
+        in_specs=[pl.BlockSpec(memory_space=pltpu.HBM)] * 8,
         out_specs=(vmem,) * 4,
         scratch_shapes=[
+            V((3, width), F32), V((3, width), F32), V((1, width), F32), V((1, width), F32), V((1, width), F32),
+            pltpu.SMEM((1, 1, slots), jnp.int32), pltpu.SMEM((1, 1, slots), jnp.int32),
+            pltpu.SMEM((1, 1), jnp.int32),
             V((CPD, 24, C), F32), V((CPD, 24, C), F32), V((CPD, 8, C), F32), V((CPD, 8, C), F32),
-            V((5, 8, C), F32), V((24, C), F32), V((16, C), F32), V((16, C), F32),
+            V((5, 8, C), F32), V((24, C), F32), V((16, C), F32), V((16, C), F32), V((C, C), F32),
             V((slots, C, C), BF16), V((slots, C, C), BF16), V((slots, 24, C), F32), V((slots, 8, C), F32),
             V((ITERS, n_tgt, 8, C), F32), V((ITERS, Y_HI, 8, C), F32), V((ITERS, n_z, 8, C), F32),
             V((24, C), F32), V((Y_HI, 24, C // Y_HI), F32), V((n_z, 24, C // Y_HI), F32),
             V((Y_HI, 24, C // Y_HI), F32), V((n_tgt, 4, share), F32), V((n_tgt, 4, share), F32),
-            pltpu.SemaphoreType.DMA((10,)), pltpu.SemaphoreType.DMA((10,)),
+            pltpu.SemaphoreType.DMA((8,)), pltpu.SemaphoreType.DMA((10,)), pltpu.SemaphoreType.DMA((10,)),
         ],
         compiler_params=pltpu.CompilerParams(collective_id=0, has_side_effects=True,
-                                             vmem_limit_bytes=40 * 1024 * 1024),
+                                             vmem_limit_bytes=56 * 1024 * 1024),
         name="sinkhorn",
     )(x, y, a.reshape(1, -1), b.reshape(1, -1), g.reshape(1, -1), ts, tt, tc)
+    f, g1, sg, tg = hand_out(f, g1, sg, tg)
     return f.reshape(-1), g1.reshape(-1), sg, tg
 
 

time: 90.2 us -> 69.8 us (0.77)
  Pallas kernels: 81.4 us -> 67.3 us
  local copies, waits for them, and re-layouts: 6.92 us -> 0 us
    pallas_call x1, Pallas kernels: 81.4 us -> 63.1 us  [body(): pl.pallas_call(functools.partial(kernel, n_src, n_tgt, slots, C), out_sha...]
    unnamed x18 -> x0, local copies, waits for them, and re-layouts: 6.92 us -> none
    pallas_call x0 -> x1, Pallas kernels: none -> 4.24 us  [hand_out(): pl.pallas_call(copy_kernel, out_shape=tuple((jax.ShapeDtypeStruct(a.shape...]
where the time goes in v2:
time: 69.8 us; the launch traced here: 68.6 us
  Pallas kernels  67.3 us (96%)
  between operations  1.29 us (2%)
    pallas_call x1, Pallas kernels, body(): pl.pallas_call(functools.partial(kernel, n_src, n_tgt, slots, C), out_sha...  63.1 us
    pallas_call x1, Pallas kernels, hand_out(): pl.pallas_call(copy_kernel, out_shape=tuple((jax.ShapeDtypeStruct(a.shape...  4.24 us

profile of v2, /device:TPU:6, one launch (start us, length us, event | category | flops | bytes accessed | tf_op | source)
XLA Modules:
  0.0 68.6 jit_solution(15153527832225708673)
XLA Ops:
  1.3 63.1 %sinkhorn.1 = (f32[1,4096]{1,0:T(1,128)}, f32[1,4096]{1,0:T(1,128)}, f32[3,256]{1,0:T(4,128)}, f32[3,4096]{1,0:T(4,128)}) custom-call(f32[3,4096]{1,0:T(4,128)} %refs_0_.1, f32[3,4096]{1,0:T(4,128)} %refs_1_.1, f32[1,4096]{1,0:T(1,128)} %bitcast.5, f32[1,4096]{1,0:T(1,128)} %bitcast.6, f32[1,4096]{1,0:T(1,128)} %bitcast.7, s32[1,1,12]{2,1,0:T(1,128)} %refs_5_.1, ...), custom_call_target="tpu_custom_call" | custom-call | tf_op jit(solution)/shard_map/sinkhorn/pallas_call | solution.py:355
  64.4 4.2 %hand_out.1 = (f32[1,4096]{1,0:T(1,128)}, f32[1,4096]{1,0:T(1,128)}, f32[3,256]{1,0:T(4,128)}, f32[3,4096]{1,0:T(4,128)}) custom-call(f32[1,4096]{1,0:T(1,128)} %get-tuple-element.12.refs_0_, f32[1,4096]{1,0:T(1,128)} %get-tuple-element.13.refs_1_, f32[3,256]{1,0:T(4,128)} %get-tuple-element.14.refs_2_, f32[3,4096]{1,0:T(4,128)} %get-tuple-element.15.refs_3_), custom_call_target="tpu_custom_call" | custom-call | tf_op jit(solution)/shard_map/hand_out/pallas_call | solution.py:334

commit v3 on v2

--- a/solution.py
+++ b/solution.py
@@ -34,14 +34,16 @@
 
 def kernel(n_src, n_tgt, slots, C, *refs):
     ins, refs = refs[:8], refs[8:]
+    outs, refs = refs[:4], refs[4:]
+    held, refs = refs[:8], refs[8:]
     (f_out, g_out, sg_out, tg_out), refs = refs[:4], refs[4:]
-    held, refs = refs[:8], refs[8:]
-    (xs, ys, xt, yt, cl, bias, tops, sums, held_scores, ehi, elo, tx, gs,
-     rbuf, ybuf, zbuf, xbar, xybuf, xzbuf, xtbuf, dsend, dbuf, insem, ssem, rsem) = refs
+    (xs, ys, xt, yt, cl, bias, tops, sums, held_scores, exps, ehi, elo, tx, gs,
+     rbuf, ybuf, zbuf, xbar, xybuf, xzbuf, xtbuf, dsend, dbuf, insem, outsem, ssem, rsem) = refs
     x_ref, y_ref, a_ref, b_ref, g_ref, ts_ref, tt_ref, tc_ref = held
     fetches = [pltpu.make_async_copy(ins[k], held[k], insem.at[k]) for k in range(8)]
     for fetch in fetches:
         fetch.start()
+    stores = [pltpu.make_async_copy((f_out, g_out, sg_out, tg_out)[k], outs[k], outsem.at[k]) for k in range(4)]
     n_z = n_src // Y_HI
     s = lax.axis_index("src")
     t = lax.axis_index("tgt")
@@ -116,7 +118,7 @@
         bias[8:16, :] = two
         bias[16:24, :] = three
 
-    def one_pass(value, summed, own, summed_ref, own_ref):
+    def one_pass(value, summed, own, summed_ref, own_ref, keep=False):
         set_bias(value)
 
         def scores_of(k):
@@ -125,9 +127,12 @@
             return jnp.max(scores, axis=0, keepdims=True)
 
         def tile(k, top):
-            acc = jnp.exp2(held_scores[0:16, :] - top)
-            for i in range(16, C, 16):
-                acc = acc + jnp.exp2(held_scores[i:i + 16, :] - top)
+            acc = None
+            for i in range(0, C, 16):
+                e = jnp.exp2(held_scores[i:i + 16, :] - top)
+                if keep:
+                    exps[k, i:i + 16, :] = e
+                acc = e if acc is None else acc + e
             tops[pl.ds(k, 1), :] = top
             sums[pl.ds(k, 1), :] = jnp.sum(acc, axis=0, keepdims=True)
             return scores_of(jnp.minimum(k + 1, slots - 1))
@@ -192,24 +197,20 @@
     one_pass(cl[1] + v, ys, xs, tt_ref, ts_ref)
     u = over_tgt(1, merge(ts_ref)[0])
 
-    one_pass(cl[0] + u, xs, ys, ts_ref, tt_ref)
+    one_pass(cl[0] + u, xs, ys, ts_ref, tt_ref, keep=True)
     local, scales, _ = merge(tt_ref)
     over_y(1, local)
 
     def mean_tile(k, carry):
         p = ts_ref[0, 0, k]
-        e = jnp.exp2(tile_scores(xs, ys, p, tt_ref[0, 0, k]) - tops[pl.ds(k, 1), :])
+        e = exps[k]
         big = e.astype(BF16)
         small = (e - big.astype(F32)).astype(BF16)
         lhs = xs[p].astype(BF16)
         tx[k] = jnp.dot(lhs, big, preferred_element_type=F32) + jnp.dot(lhs, small, preferred_element_type=F32)
         return carry
 
-    first = max(slots - 4, 0) // 4 * 4
-    lax.fori_loop(0, first, mean_tile, 0, unroll=4)
-    both = over_y_done(1)
-    over_z(1, both)
-    lax.fori_loop(first, slots, mean_tile, 0, unroll=4)
+    lax.fori_loop(0, slots, mean_tile, 0, unroll=4)
 
     per = 1.0 / functools.reduce(jnp.add, [scales[k] * tx[k, 6:7, :] for k in range(slots)])
     for c in range(3):
@@ -226,6 +227,9 @@
     xybuf[h] = xbar[:, lanes(h)]
     for at, peer in zip(y_at, y_peers):
         send(6, xbar.at[:, lanes(at)], xybuf.at[h], peer)
+
+    both = over_y_done(1)
+    over_z(1, both)
 
     row8_one = jnp.where(row8 < 3, 1.0, 0.0)
     blank = jnp.zeros((8, C), F32)
@@ -246,6 +250,7 @@
     f_all = (u + cl[3]) * BACK
     for c in range(CPD):
         f_out[:, c * C:(c + 1) * C] = f_all[c:c + 1, :]
+    stores[0].start()
     done = waiter(6, xybuf.at[pl.ds(0, Y_HI - 1)])
     done.wait_recv()
     done.wait_send()
@@ -301,12 +306,14 @@
     g_all = (cl[2] + cl[4]) * BACK
     for c in range(CPD):
         g_out[:, c * C:(c + 1) * C] = g_all[c:c + 1, :]
+    stores[1].start()
 
     done = waiter(8, dbuf.at[pl.ds(0, n_tgt - 1)])
     done.wait_recv()
     done.wait_send()
     grad = functools.reduce(jnp.add, [dbuf[k] for k in range(n_tgt)])
     sg_out[...] = grad[0:3, :]
+    stores[2].start()
 
     done = waiter(9, xtbuf.at[pl.ds(0, Y_HI - 1)])
     done.wait_recv()
@@ -317,16 +324,23 @@
             at = pl.ds(q * C + k * W, W)
             mean = jnp.concatenate([block[8 * c + q:8 * c + q + 1, :] for c in range(3)], 0)
             tg_out[:, at] = b_ref[:, at] * (y_ref[:, at] - mean)
+    stores[3].start()
+    for store in stores:
+        store.wait()
 
 
 def copy_kernel(*refs):
-    n = len(refs) // 2
+    n = (len(refs) - 1) // 3
     sem = refs[-1]
-    copies = [pltpu.make_async_copy(refs[k], refs[n + k], sem.at[k]) for k in range(n)]
-    for copy in copies:
-        copy.start()
-    for copy in copies:
-        copy.wait()
+    loads = [pltpu.make_async_copy(refs[k], refs[2 * n + k], sem.at[k]) for k in range(n)]
+    stores = [pltpu.make_async_copy(refs[2 * n + k], refs[n + k], sem.at[n + k]) for k in range(n)]
+    for load in loads:
+        load.start()
+    for load, store in zip(loads, stores):
+        load.wait()
+        store.start()
+    for store in stores:
+        store.wait()
 
 
 def hand_out(*arrays):
@@ -336,7 +350,7 @@
         out_shape=tuple(jax.ShapeDtypeStruct(a.shape, a.dtype) for a in arrays),
         in_specs=[pl.BlockSpec(memory_space=pltpu.HBM)] * n,
         out_specs=(pl.BlockSpec(memory_space=pltpu.HBM),) * n,
-        scratch_shapes=[pltpu.SemaphoreType.DMA((n,))],
+        scratch_shapes=[pltpu.VMEM(a.shape, a.dtype) for a in arrays] + [pltpu.SemaphoreType.DMA((2 * n,))],
         compiler_params=pltpu.CompilerParams(vmem_limit_bytes=56 * 1024 * 1024),
         name="hand_out",
     )(*arrays)
@@ -350,25 +364,25 @@
     C = width // CPD
     share = width // n_tgt
     n_z = n_src // Y_HI
-    vmem = pl.BlockSpec(memory_space=pltpu.VMEM)
     V = pltpu.VMEM
     f, g1, sg, tg = pl.pallas_call(
         functools.partial(kernel, n_src, n_tgt, slots, C),
         out_shape=(jax.ShapeDtypeStruct((1, width), F32), jax.ShapeDtypeStruct((1, width), F32),
                    jax.ShapeDtypeStruct((3, share), F32), jax.ShapeDtypeStruct((3, width), F32)),
         in_specs=[pl.BlockSpec(memory_space=pltpu.HBM)] * 8,
-        out_specs=(vmem,) * 4,
+        out_specs=(pl.BlockSpec(memory_space=pltpu.HBM),) * 4,
         scratch_shapes=[
             V((3, width), F32), V((3, width), F32), V((1, width), F32), V((1, width), F32), V((1, width), F32),
             pltpu.SMEM((1, 1, slots), jnp.int32), pltpu.SMEM((1, 1, slots), jnp.int32),
             pltpu.SMEM((1, 1), jnp.int32),
+            V((1, width), F32), V((1, width), F32), V((3, share), F32), V((3, width), F32),
             V((CPD, 24, C), F32), V((CPD, 24, C), F32), V((CPD, 8, C), F32), V((CPD, 8, C), F32),
             V((5, 8, C), F32), V((24, C), F32), V((16, C), F32), V((16, C), F32), V((C, C), F32),
-            V((slots, C, C), BF16), V((slots, C, C), BF16), V((slots, 24, C), F32), V((slots, 8, C), F32),
+            V((slots, C, C), F32), V((slots, C, C), BF16), V((slots, C, C), BF16), V((slots, 24, C), F32), V((slots, 8, C), F32),
             V((ITERS, n_tgt, 8, C), F32), V((ITERS, Y_HI, 8, C), F32), V((ITERS, n_z, 8, C), F32),
             V((24, C), F32), V((Y_HI, 24, C // Y_HI), F32), V((n_z, 24, C // Y_HI), F32),
             V((Y_HI, 24, C // Y_HI), F32), V((n_tgt, 4, share), F32), V((n_tgt, 4, share), F32),
-            pltpu.SemaphoreType.DMA((8,)), pltpu.SemaphoreType.DMA((10,)), pltpu.SemaphoreType.DMA((10,)),
+            pltpu.SemaphoreType.DMA((8,)), pltpu.SemaphoreType.DMA((4,)), pltpu.SemaphoreType.DMA((10,)), pltpu.SemaphoreType.DMA((10,)),
         ],
         compiler_params=pltpu.CompilerParams(collective_id=0, has_side_effects=True,
                                              vmem_limit_bytes=56 * 1024 * 1024),

time: 69.8 us -> 64.6 us (0.926); the launches traced: 68.6 us -> 64.1 us
  Pallas kernels: 67.3 us -> 62.9 us
    pallas_call x1, Pallas kernels: 4.24 us -> 1.58 us  [hand_out(): pl.pallas_call(copy_kernel, out_shape=tuple((jax.ShapeDtypeStruct(a.shape...]
    pallas_call x1, Pallas kernels: 63.1 us -> 61.3 us  [body(): pl.pallas_call(functools.partial(kernel, n_src, n_tgt, slots, C), out_sha...]
where the time goes in v3:
time: 64.6 us; the launch traced here: 64.1 us
  Pallas kernels  62.9 us (97%)
  between operations  1.29 us (2%)
    pallas_call x1, Pallas kernels, body(): pl.pallas_call(functools.partial(kernel, n_src, n_tgt, slots, C), out_sha...  61.3 us
    pallas_call x1, Pallas kernels, hand_out(): pl.pallas_call(copy_kernel, out_shape=tuple((jax.ShapeDtypeStruct(a.shape...  1.58 us

profile of v3, /device:TPU:6, one launch (start us, length us, event | category | flops | bytes accessed | tf_op | source)
XLA Modules:
  0.0 64.1 jit_solution(918647730314170100)
XLA Ops:
  1.3 61.3 %sinkhorn.1 = (f32[1,4096]{1,0:T(1,128)}, f32[1,4096]{1,0:T(1,128)}, f32[3,256]{1,0:T(4,128)}, f32[3,4096]{1,0:T(4,128)}) custom-call(f32[3,4096]{1,0:T(4,128)} %refs_0_.1, f32[3,4096]{1,0:T(4,128)} %refs_1_.1, f32[1,4096]{1,0:T(1,128)} %bitcast.5, f32[1,4096]{1,0:T(1,128)} %bitcast.6, f32[1,4096]{1,0:T(1,128)} %bitcast.7, s32[1,1,12]{2,1,0:T(1,128)} %refs_5_.1, ...), custom_call_target="tpu_custom_call" | custom-call | tf_op jit(solution)/shard_map/sinkhorn/pallas_call | solution.py:368
  62.6 1.6 %hand_out.1 = (f32[1,4096]{1,0:T(1,128)}, f32[1,4096]{1,0:T(1,128)}, f32[3,256]{1,0:T(4,128)}, f32[3,4096]{1,0:T(4,128)}) custom-call(f32[1,4096]{1,0:T(1,128)} %get-tuple-element.12.refs_0_, f32[1,4096]{1,0:T(1,128)} %get-tuple-element.13.refs_1_, f32[3,256]{1,0:T(4,128)} %get-tuple-element.14.refs_2_, f32[3,4096]{1,0:T(4,128)} %get-tuple-element.15.refs_3_), custom_call_target="tpu_custom_call" | custom-call | tf_op jit(solution)/shard_map/hand_out/pallas_call | solution.py:348

commit v4 on v3

--- a/solution.py
+++ b/solution.py
@@ -37,7 +37,7 @@
     outs, refs = refs[:4], refs[4:]
     held, refs = refs[:8], refs[8:]
     (f_out, g_out, sg_out, tg_out), refs = refs[:4], refs[4:]
-    (xs, ys, xt, yt, cl, bias, tops, sums, held_scores, exps, ehi, elo, tx, gs,
+    (xs, ys, xt, yt, cl, bias, tops, sums, held_scores, columns, row_scores, col_scores, ehi, elo, tx, gs,
      rbuf, ybuf, zbuf, xbar, xybuf, xzbuf, xtbuf, dsend, dbuf, insem, outsem, ssem, rsem) = refs
     x_ref, y_ref, a_ref, b_ref, g_ref, ts_ref, tt_ref, tc_ref = held
     fetches = [pltpu.make_async_copy(ins[k], held[k], insem.at[k]) for k in range(8)]
@@ -118,25 +118,65 @@
         bias[8:16, :] = two
         bias[16:24, :] = three
 
-    def one_pass(value, summed, own, summed_ref, own_ref, keep=False):
+    def first_pass(value):
         set_bias(value)
 
         def scores_of(k):
-            scores = tile_scores(summed, own, summed_ref[0, 0, k], own_ref[0, 0, k])
+            scores = tile_scores(ys, xs, tt_ref[0, 0, k], ts_ref[0, 0, k])
             held_scores[...] = scores
             return jnp.max(scores, axis=0, keepdims=True)
 
         def tile(k, top):
             acc = None
             for i in range(0, C, 16):
-                e = jnp.exp2(held_scores[i:i + 16, :] - top)
-                if keep:
-                    exps[k, i:i + 16, :] = e
+                part = held_scores[i:i + 16, :]
+                row_scores[k, i:i + 16, :] = part
+                e = jnp.exp2(part - top)
                 acc = e if acc is None else acc + e
             tops[pl.ds(k, 1), :] = top
             sums[pl.ds(k, 1), :] = jnp.sum(acc, axis=0, keepdims=True)
             return scores_of(jnp.minimum(k + 1, slots - 1))
         lax.fori_loop(0, slots, tile, scores_of(0), unroll=4)
+
+    def kept_pass(value, scores, summed_ref, keep=None):
+        turned = value.T
+        for c in range(CPD):
+            columns[c] = jnp.broadcast_to(turned[:, c:c + 1], (C, 128))
+
+        def exps_at(k, i, top, acc):
+            e = jnp.exp2(held_scores[i:i + 8, :] - top)
+            if keep is not None:
+                keep[k, i:i + 8, :] = e
+            return e if acc is None else acc + e
+
+        def biased_at(k, c, i, most):
+            column = columns[c, i:i + 8, :]
+            v = scores[k, i:i + 8, :] + jnp.concatenate([column] * (C // 128), 1)
+            held_scores[i:i + 8, :] = v
+            return v if most is None else jnp.maximum(most, v)
+
+        def put(k, top, acc):
+            tops[pl.ds(k, 1), :] = top
+            sums[pl.ds(k, 1), :] = jnp.sum(acc, axis=0, keepdims=True)
+
+        def tile(k, top):
+            c = summed_ref[0, 0, k + 1]
+            acc = most = None
+            for i in range(0, C, 8):
+                acc = exps_at(k, i, top, acc)
+                most = biased_at(k + 1, c, i, most)
+            put(k, top, acc)
+            return jnp.max(most, axis=0, keepdims=True)
+
+        c = summed_ref[0, 0, 0]
+        most = None
+        for i in range(0, C, 8):
+            most = biased_at(0, c, i, most)
+        top = lax.fori_loop(0, slots - 1, tile, jnp.max(most, axis=0, keepdims=True))
+        acc = None
+        for i in range(0, C, 8):
+            acc = exps_at(slots - 1, i, top, acc)
+        put(slots - 1, top, acc)
 
     def merge(own_ref):
         own = owners(own_ref)
@@ -153,6 +193,9 @@
         buf[t] = local
         for peer in tgt_peers:
             send(turn, buf.at[t], buf.at[t], peer)
+
+    def over_tgt_done(turn):
+        buf = rbuf.at[turn]
         done = waiter(turn, buf.at[pl.ds(0, n_tgt - 1)])
         done.wait_recv()
         done.wait_send()
@@ -185,19 +228,28 @@
             done.wait_send()
         return logsum([buf[k] for k in range(n_z)])
 
-    one_pass(cl[1] + v, ys, xs, tt_ref, ts_ref)
+    first_pass(cl[1] + v)
+    start = v
     local = merge(ts_ref)[0]
     pl.semaphore_wait(barrier, len(everyone))
-    u = over_tgt(0, local)
-    one_pass(cl[0] + u, xs, ys, ts_ref, tt_ref)
+    over_tgt(0, local)
+
+    def score_tile(k, carry):
+        col_scores[k] = lax.dot_general(xs[ts_ref[0, 0, k]].astype(BF16), ys[tt_ref[0, 0, k]].astype(BF16),
+                                        (((0,), (0,)), ((), ())), preferred_element_type=F32)
+        return carry
+    lax.fori_loop(0, slots, score_tile, 0, unroll=4)
+    u = over_tgt_done(0)
+    kept_pass(cl[0] + u, col_scores, ts_ref)
     over_y(0, merge(tt_ref)[0])
     over_z(0, over_y_done(0))
     v = -over_z_done(0)
 
-    one_pass(cl[1] + v, ys, xs, tt_ref, ts_ref)
-    u = over_tgt(1, merge(ts_ref)[0])
-
-    one_pass(cl[0] + u, xs, ys, ts_ref, tt_ref, keep=True)
+    kept_pass(v - start, row_scores, tt_ref)
+    over_tgt(1, merge(ts_ref)[0])
+    u = over_tgt_done(1)
+    exps = row_scores
+    kept_pass(cl[0] + u, col_scores, ts_ref, keep=exps)
     local, scales, _ = merge(tt_ref)
     over_y(1, local)
 
@@ -231,6 +283,7 @@
     both = over_y_done(1)
     over_z(1, both)
 
+    set_bias(cl[0] + u)
     row8_one = jnp.where(row8 < 3, 1.0, 0.0)
     blank = jnp.zeros((8, C), F32)
 
@@ -377,7 +430,7 @@
             pltpu.SMEM((1, 1), jnp.int32),
             V((1, width), F32), V((1, width), F32), V((3, share), F32), V((3, width), F32),
             V((CPD, 24, C), F32), V((CPD, 24, C), F32), V((CPD, 8, C), F32), V((CPD, 8, C), F32),
-            V((5, 8, C), F32), V((24, C), F32), V((16, C), F32), V((16, C), F32), V((C, C), F32),
+            V((5, 8, C), F32), V((24, C), F32), V((16, C), F32), V((16, C), F32), V((C, C), F32), V((CPD, C, 128), F32), V((slots, C, C), F32),
             V((slots, C, C), F32), V((slots, C, C), BF16), V((slots, C, C), BF16), V((slots, 24, C), F32), V((slots, 8, C), F32),
             V((ITERS, n_tgt, 8, C), F32), V((ITERS, Y_HI, 8, C), F32), V((ITERS, n_z, 8, C), F32),
             V((24, C), F32), V((Y_HI, 24, C // Y_HI), F32), V((n_z, 24, C // Y_HI), F32),

time: 64.6 us -> 66 us (1.022)
  Pallas kernels: 62.9 us -> 64.5 us
    pallas_call x1, Pallas kernels: 61.3 us -> 62.9 us  [body(): pl.pallas_call(functools.partial(kernel, n_src, n_tgt, slots, C), out_sha...]
where the time goes in v4:
time: 66 us; the launch traced here: 65.8 us
  Pallas kernels  64.5 us (98%)
  between operations  1.29 us (2%)
    pallas_call x1, Pallas kernels, body(): pl.pallas_call(functools.partial(kernel, n_src, n_tgt, slots, C), out_sha...  62.9 us
    pallas_call x1, Pallas kernels, hand_out(): pl.pallas_call(copy_kernel, out_shape=tuple((jax.ShapeDtypeStruct(a.shape...  1.58 us

profile of v4, /device:TPU:6, one launch (start us, length us, event | category | flops | bytes accessed | tf_op | source)
XLA Modules:
  0.0 65.8 jit_solution(9794902486595035336)
XLA Ops:
  1.3 62.9 %sinkhorn.1 = (f32[1,4096]{1,0:T(1,128)}, f32[1,4096]{1,0:T(1,128)}, f32[3,256]{1,0:T(4,128)}, f32[3,4096]{1,0:T(4,128)}) custom-call(f32[3,4096]{1,0:T(4,128)} %refs_0_.1, f32[3,4096]{1,0:T(4,128)} %refs_1_.1, f32[1,4096]{1,0:T(1,128)} %bitcast.5, f32[1,4096]{1,0:T(1,128)} %bitcast.6, f32[1,4096]{1,0:T(1,128)} %bitcast.7, s32[1,1,12]{2,1,0:T(1,128)} %refs_5_.1, ...), custom_call_target="tpu_custom_call" | custom-call | tf_op jit(solution)/shard_map/sinkhorn/pallas_call | solution.py:421
  64.2 1.6 %hand_out.1 = (f32[1,4096]{1,0:T(1,128)}, f32[1,4096]{1,0:T(1,128)}, f32[3,256]{1,0:T(4,128)}, f32[3,4096]{1,0:T(4,128)}) custom-call(f32[1,4096]{1,0:T(1,128)} %get-tuple-element.12.refs_0_, f32[1,4096]{1,0:T(1,128)} %get-tuple-element.13.refs_1_, f32[3,256]{1,0:T(4,128)} %get-tuple-element.14.refs_2_, f32[3,4096]{1,0:T(4,128)} %get-tuple-element.15.refs_3_), custom_call_target="tpu_custom_call" | custom-call | tf_op jit(solution)/shard_map/hand_out/pallas_call | solution.py:401

commit v5 on v4

--- a/solution.py
+++ b/solution.py
@@ -139,9 +139,11 @@
         lax.fori_loop(0, slots, tile, scores_of(0), unroll=4)
 
     def kept_pass(value, scores, summed_ref, keep=None):
-        turned = value.T
-        for c in range(CPD):
-            columns[c] = jnp.broadcast_to(turned[:, c:c + 1], (C, 128))
+        bias[0:8, :] = value
+
+        def turn(k):
+            row = bias[pl.ds(summed_ref[0, 0, k], 1), :]
+            columns[...] = jnp.broadcast_to(row, (128, C)).T
 
         def exps_at(k, i, top, acc):
             e = jnp.exp2(held_scores[i:i + 8, :] - top)
@@ -149,8 +151,8 @@
                 keep[k, i:i + 8, :] = e
             return e if acc is None else acc + e
 
-        def biased_at(k, c, i, most):
-            column = columns[c, i:i + 8, :]
+        def biased_at(k, i, most):
+            column = columns[i:i + 8, :]
             v = scores[k, i:i + 8, :] + jnp.concatenate([column] * (C // 128), 1)
             held_scores[i:i + 8, :] = v
             return v if most is None else jnp.maximum(most, v)
@@ -160,18 +162,19 @@
             sums[pl.ds(k, 1), :] = jnp.sum(acc, axis=0, keepdims=True)
 
         def tile(k, top):
-            c = summed_ref[0, 0, k + 1]
             acc = most = None
             for i in range(0, C, 8):
                 acc = exps_at(k, i, top, acc)
-                most = biased_at(k + 1, c, i, most)
+                most = biased_at(k + 1, i, most)
+            turn(jnp.minimum(k + 2, slots - 1))
             put(k, top, acc)
             return jnp.max(most, axis=0, keepdims=True)
 
-        c = summed_ref[0, 0, 0]
+        turn(0)
         most = None
         for i in range(0, C, 8):
-            most = biased_at(0, c, i, most)
+            most = biased_at(0, i, most)
+        turn(1)
         top = lax.fori_loop(0, slots - 1, tile, jnp.max(most, axis=0, keepdims=True))
         acc = None
         for i in range(0, C, 8):
@@ -335,6 +338,14 @@
         return carry
     lax.fori_loop(0, slots, grad_tile, 0, unroll=4)
 
+    if n_z > 1:
+        done = waiter(7, xzbuf.at[pl.ds(0, n_z - 1)])
+        done.wait_recv()
+        done.wait_send()
+    xtbuf[h] = weighted(xzbuf, zbuf.at[1], n_z, -cl[2, :, lanes(h)])
+    for peer in y_peers:
+        send(9, xtbuf.at[h], xtbuf.at[h], peer)
+
     own = owners(ts_ref)
     share = CPD * C // n_tgt
     per_cluster = C // share
@@ -349,13 +360,6 @@
     for at, peer in zip(tgt_at, tgt_peers):
         send(8, dsend.at[at], dbuf.at[t], peer)
 
-    if n_z > 1:
-        done = waiter(7, xzbuf.at[pl.ds(0, n_z - 1)])
-        done.wait_recv()
-        done.wait_send()
-    xtbuf[h] = weighted(xzbuf, zbuf.at[1], n_z, -cl[2, :, lanes(h)])
-    for peer in y_peers:
-        send(9, xtbuf.at[h], xtbuf.at[h], peer)
     g_all = (cl[2] + cl[4]) * BACK
     for c in range(CPD):
         g_out[:, c * C:(c + 1) * C] = g_all[c:c + 1, :]
@@ -430,7 +434,7 @@
             pltpu.SMEM((1, 1), jnp.int32),
             V((1, width), F32), V((1, width), F32), V((3, share), F32), V((3, width), F32),
             V((CPD, 24, C), F32), V((CPD, 24, C), F32), V((CPD, 8, C), F32), V((CPD, 8, C), F32),
-            V((5, 8, C), F32), V((24, C), F32), V((16, C), F32), V((16, C), F32), V((C, C), F32), V((CPD, C, 128), F32), V((slots, C, C), F32),
+            V((5, 8, C), F32), V((24, C), F32), V((16, C), F32), V((16, C), F32), V((C, C), F32), V((C, 128), F32), V((slots, C, C), F32),
             V((slots, C, C), F32), V((slots, C, C), BF16), V((slots, C, C), BF16), V((slots, 24, C), F32), V((slots, 8, C), F32),
             V((ITERS, n_tgt, 8, C), F32), V((ITERS, Y_HI, 8, C), F32), V((ITERS, n_z, 8, C), F32),
             V((24, C), F32), V((Y_HI, 24, C // Y_HI), F32), V((n_z, 24, C // Y_HI), F32),

time: 66 us -> 64.2 us (0.973)
  Pallas kernels: 64.5 us -> 62.7 us
    pallas_call x1, Pallas kernels: 62.9 us -> 61.1 us  [body(): pl.pallas_call(functools.partial(kernel, n_src, n_tgt, slots, C), out_sha...]
where the time goes in v5:
time: 64.2 us; the launch traced here: 63.9 us
  Pallas kernels  62.7 us (98%)
  between operations  1.29 us (2%)
    pallas_call x1, Pallas kernels, body(): pl.pallas_call(functools.partial(kernel, n_src, n_tgt, slots, C), out_sha...  61.1 us
    pallas_call x1, Pallas kernels, hand_out(): pl.pallas_call(copy_kernel, out_shape=tuple((jax.ShapeDtypeStruct(a.shape...  1.58 us

profile of v5, /device:TPU:6, one launch (start us, length us, event | category | flops | bytes accessed | tf_op | source)
XLA Modules:
  0.0 63.9 jit_solution(9132946465804044083)
XLA Ops:
  1.3 61.1 %sinkhorn.1 = (f32[1,4096]{1,0:T(1,128)}, f32[1,4096]{1,0:T(1,128)}, f32[3,256]{1,0:T(4,128)}, f32[3,4096]{1,0:T(4,128)}) custom-call(f32[3,4096]{1,0:T(4,128)} %refs_0_.1, f32[3,4096]{1,0:T(4,128)} %refs_1_.1, f32[1,4096]{1,0:T(1,128)} %bitcast.5, f32[1,4096]{1,0:T(1,128)} %bitcast.6, f32[1,4096]{1,0:T(1,128)} %bitcast.7, s32[1,1,12]{2,1,0:T(1,128)} %refs_5_.1, ...), custom_call_target="tpu_custom_call" | custom-call | tf_op jit(solution)/shard_map/sinkhorn/pallas_call | solution.py:425
  62.4 1.6 %hand_out.1 = (f32[1,4096]{1,0:T(1,128)}, f32[1,4096]{1,0:T(1,128)}, f32[3,256]{1,0:T(4,128)}, f32[3,4096]{1,0:T(4,128)}) custom-call(f32[1,4096]{1,0:T(1,128)} %get-tuple-element.12.refs_0_, f32[1,4096]{1,0:T(1,128)} %get-tuple-element.13.refs_1_, f32[3,256]{1,0:T(4,128)} %get-tuple-element.14.refs_2_, f32[3,4096]{1,0:T(4,128)} %get-tuple-element.15.refs_3_), custom_call_target="tpu_custom_call" | custom-call | tf_op jit(solution)/shard_map/hand_out/pallas_call | solution.py:405

commit v6 on v4

--- a/solution.py
+++ b/solution.py
@@ -74,10 +74,13 @@
         return pltpu.make_async_remote_copy(src_ref=like, dst_ref=like, send_sem=ssem.at[no], recv_sem=rsem.at[no],
                                             device_id=everyone[0], device_id_type=MESH)
 
-    for fetch in fetches:
-        fetch.wait()
+    for k in (0, 1, 3, 4, 5, 6, 7):
+        fetches[k].wait()
     row8 = lax.broadcasted_iota(jnp.int32, (8, C), 0)
     row24 = lax.rem(lax.broadcasted_iota(jnp.int32, (24, C), 0), 8)
+    def half_norm(v):
+        return 0.5 * jnp.sum(jnp.where(row8 < 3, v * v, 0.0), axis=0, keepdims=True)
+
     for c in range(CPD):
         at = pl.ds(c * C, C)
         for ref, full, stat, norm, ones in ((x_ref, xt, xs, 3, 1.0), (y_ref, yt, ys, 4, 0.0)):
@@ -93,11 +96,9 @@
                 stat[c] = jnp.concatenate([a, jnp.where(row8 < 3, one, two), jnp.where(row8 < 3, one, three)], 0)
             else:
                 stat[c] = jnp.concatenate([one, two, jnp.where(row8 < 3, three, one)], 0)
-            cl[norm, c:c + 1, :] = 0.5 * jnp.sum(jnp.where(row8 < 3, v * v, 0.0), axis=0, keepdims=True)
-        cl[0, c:c + 1, :] = a_ref[:, at]
+                cl[norm, c:c + 1, :] = half_norm(v)
         cl[1, c:c + 1, :] = b_ref[:, at]
         cl[2, c:c + 1, :] = g_ref[:, at]
-    cl[0] = jnp.log2(cl[0])
     cl[1] = jnp.log2(cl[1])
     v = cl[2] * (1.0 / BACK) - cl[4]
 
@@ -139,9 +140,8 @@
         lax.fori_loop(0, slots, tile, scores_of(0), unroll=4)
 
     def kept_pass(value, scores, summed_ref, keep=None):
-        turned = value.T
         for c in range(CPD):
-            columns[c] = jnp.broadcast_to(turned[:, c:c + 1], (C, 128))
+            columns[c] = jnp.broadcast_to(value[c:c + 1, :], (128, C)).T
 
         def exps_at(k, i, top, acc):
             e = jnp.exp2(held_scores[i:i + 8, :] - top)
@@ -239,6 +239,11 @@
                                         (((0,), (0,)), ((), ())), preferred_element_type=F32)
         return carry
     lax.fori_loop(0, slots, score_tile, 0, unroll=4)
+    fetches[2].wait()
+    for c in range(CPD):
+        cl[0, c:c + 1, :] = a_ref[:, c * C:(c + 1) * C]
+        cl[3, c:c + 1, :] = half_norm(xt[c])
+    cl[0] = jnp.log2(cl[0])
     u = over_tgt_done(0)
     kept_pass(cl[0] + u, col_scores, ts_ref)
     over_y(0, merge(tt_ref)[0])
@@ -258,7 +263,7 @@
         e = exps[k]
         big = e.astype(BF16)
         small = (e - big.astype(F32)).astype(BF16)
-        lhs = xs[p].astype(BF16)
+        lhs = jnp.concatenate([xs[p, 0:8, :], xs[p, 16:24, :]], 0).astype(BF16)
         tx[k] = jnp.dot(lhs, big, preferred_element_type=F32) + jnp.dot(lhs, small, preferred_element_type=F32)
         return carry
 
@@ -268,7 +273,7 @@
     for c in range(3):
         acc = jnp.zeros((8, C), F32)
         for k in range(slots):
-            rows = tx[k, c:c + 1, :] + tx[k, 3 + c:4 + c, :] + tx[k, 19 + c:20 + c, :]
+            rows = tx[k, c:c + 1, :] + tx[k, 3 + c:4 + c, :] + tx[k, 11 + c:12 + c, :]
             acc = acc + scales[k] * rows
         xbar[8 * c:8 * c + 8, :] = acc * per
     W = C // Y_HI
@@ -328,12 +333,20 @@
         q = tt_ref[0, 0, k]
         w = jnp.exp2(bias[pl.ds(q, 1), :] + tops[pl.ds(k, 1), :])
         one, two, three = split3(yt[q] * w)
-        lhs = jnp.concatenate([one, two, three], 0).astype(BF16)
+        lhs = jnp.concatenate([one, two + three], 0).astype(BF16)
         out = (jnp.dot(lhs, ehi[k], preferred_element_type=F32)
                + jnp.dot(lhs, elo[k], preferred_element_type=F32))
-        gs[k] = out[0:8, :] + out[8:16, :] + out[16:24, :]
+        gs[k] = out[0:8, :] + out[8:16, :]
         return carry
     lax.fori_loop(0, slots, grad_tile, 0, unroll=4)
+
+    if n_z > 1:
+        done = waiter(7, xzbuf.at[pl.ds(0, n_z - 1)])
+        done.wait_recv()
+        done.wait_send()
+    xtbuf[h] = weighted(xzbuf, zbuf.at[1], n_z, -cl[2, :, lanes(h)])
+    for peer in y_peers:
+        send(9, xtbuf.at[h], xtbuf.at[h], peer)
 
     own = owners(ts_ref)
     share = CPD * C // n_tgt
@@ -349,13 +362,6 @@
     for at, peer in zip(tgt_at, tgt_peers):
         send(8, dsend.at[at], dbuf.at[t], peer)
 
-    if n_z > 1:
-        done = waiter(7, xzbuf.at[pl.ds(0, n_z - 1)])
-        done.wait_recv()
-        done.wait_send()
-    xtbuf[h] = weighted(xzbuf, zbuf.at[1], n_z, -cl[2, :, lanes(h)])
-    for peer in y_peers:
-        send(9, xtbuf.at[h], xtbuf.at[h], peer)
     g_all = (cl[2] + cl[4]) * BACK
     for c in range(CPD):
         g_out[:, c * C:(c + 1) * C] = g_all[c:c + 1, :]
@@ -431,7 +437,7 @@
             V((1, width), F32), V((1, width), F32), V((3, share), F32), V((3, width), F32),
             V((CPD, 24, C), F32), V((CPD, 24, C), F32), V((CPD, 8, C), F32), V((CPD, 8, C), F32),
             V((5, 8, C), F32), V((24, C), F32), V((16, C), F32), V((16, C), F32), V((C, C), F32), V((CPD, C, 128), F32), V((slots, C, C), F32),
-            V((slots, C, C), F32), V((slots, C, C), BF16), V((slots, C, C), BF16), V((slots, 24, C), F32), V((slots, 8, C), F32),
+            V((slots, C, C), F32), V((slots, C, C), BF16), V((slots, C, C), BF16), V((slots, 16, C), F32), V((slots, 8, C), F32),
             V((ITERS, n_tgt, 8, C), F32), V((ITERS, Y_HI, 8, C), F32), V((ITERS, n_z, 8, C), F32),
             V((24, C), F32), V((Y_HI, 24, C // Y_HI), F32), V((n_z, 24, C // Y_HI), F32),
             V((Y_HI, 24, C // Y_HI), F32), V((n_tgt, 4, share), F32), V((n_tgt, 4, share), F32),

time: 66 us -> 64.9 us (0.983)
  Pallas kernels: 64.5 us -> 63.4 us
    pallas_call x1, Pallas kernels: 62.9 us -> 61.8 us  [body(): pl.pallas_call(functools.partial(kernel, n_src, n_tgt, slots, C), out_sha...]
where the time goes in v6:
time: 64.9 us; the launch traced here: 64.7 us
  Pallas kernels  63.4 us (98%)
  between operations  1.29 us (2%)
    pallas_call x1, Pallas kernels, body(): pl.pallas_call(functools.partial(kernel, n_src, n_tgt, slots, C), out_sha...  61.8 us
    pallas_call x1, Pallas kernels, hand_out(): pl.pallas_call(copy_kernel, out_shape=tuple((jax.ShapeDtypeStruct(a.shape...  1.58 us

profile of v6, /device:TPU:6, one launch (start us, length us, event | category | flops | bytes accessed | tf_op | source)
XLA Modules:
  0.0 64.7 jit_solution(10680250930123962888)
XLA Ops:
  1.3 61.8 %sinkhorn.1 = (f32[1,4096]{1,0:T(1,128)}, f32[1,4096]{1,0:T(1,128)}, f32[3,256]{1,0:T(4,128)}, f32[3,4096]{1,0:T(4,128)}) custom-call(f32[3,4096]{1,0:T(4,128)} %refs_0_.1, f32[3,4096]{1,0:T(4,128)} %refs_1_.1, f32[1,4096]{1,0:T(1,128)} %bitcast.5, f32[1,4096]{1,0:T(1,128)} %bitcast.6, f32[1,4096]{1,0:T(1,128)} %bitcast.7, s32[1,1,12]{2,1,0:T(1,128)} %refs_5_.1, ...), custom_call_target="tpu_custom_call" | custom-call | tf_op jit(solution)/shard_map/sinkhorn/pallas_call | solution.py:427
  63.1 1.6 %hand_out.1 = (f32[1,4096]{1,0:T(1,128)}, f32[1,4096]{1,0:T(1,128)}, f32[3,256]{1,0:T(4,128)}, f32[3,4096]{1,0:T(4,128)}) custom-call(f32[1,4096]{1,0:T(1,128)} %get-tuple-element.12.refs_0_, f32[1,4096]{1,0:T(1,128)} %get-tuple-element.13.refs_1_, f32[3,256]{1,0:T(4,128)} %get-tuple-element.14.refs_2_, f32[3,4096]{1,0:T(4,128)} %get-tuple-element.15.refs_3_), custom_call_target="tpu_custom_call" | custom-call | tf_op jit(solution)/shard_map/hand_out/pallas_call | solution.py:407

commit v7 on v6

--- a/solution.py
+++ b/solution.py
@@ -140,8 +140,11 @@
         lax.fori_loop(0, slots, tile, scores_of(0), unroll=4)
 
     def kept_pass(value, scores, summed_ref, keep=None):
-        for c in range(CPD):
-            columns[c] = jnp.broadcast_to(value[c:c + 1, :], (128, C)).T
+        bias[0:8, :] = value
+
+        def turn(k):
+            row = bias[pl.ds(summed_ref[0, 0, k], 1), :]
+            columns[...] = jnp.broadcast_to(row, (128, C)).T
 
         def exps_at(k, i, top, acc):
             e = jnp.exp2(held_scores[i:i + 8, :] - top)
@@ -149,8 +152,8 @@
                 keep[k, i:i + 8, :] = e
             return e if acc is None else acc + e
 
-        def biased_at(k, c, i, most):
-            column = columns[c, i:i + 8, :]
+        def biased_at(k, i, most):
+            column = columns[i:i + 8, :]
             v = scores[k, i:i + 8, :] + jnp.concatenate([column] * (C // 128), 1)
             held_scores[i:i + 8, :] = v
             return v if most is None else jnp.maximum(most, v)
@@ -160,18 +163,19 @@
             sums[pl.ds(k, 1), :] = jnp.sum(acc, axis=0, keepdims=True)
 
         def tile(k, top):
-            c = summed_ref[0, 0, k + 1]
             acc = most = None
             for i in range(0, C, 8):
                 acc = exps_at(k, i, top, acc)
-                most = biased_at(k + 1, c, i, most)
+                most = biased_at(k + 1, i, most)
+            turn(jnp.minimum(k + 2, slots - 1))
             put(k, top, acc)
             return jnp.max(most, axis=0, keepdims=True)
 
-        c = summed_ref[0, 0, 0]
+        turn(0)
         most = None
         for i in range(0, C, 8):
-            most = biased_at(0, c, i, most)
+            most = biased_at(0, i, most)
+        turn(1)
         top = lax.fori_loop(0, slots - 1, tile, jnp.max(most, axis=0, keepdims=True))
         acc = None
         for i in range(0, C, 8):
@@ -436,7 +440,7 @@
             pltpu.SMEM((1, 1), jnp.int32),
             V((1, width), F32), V((1, width), F32), V((3, share), F32), V((3, width), F32),
             V((CPD, 24, C), F32), V((CPD, 24, C), F32), V((CPD, 8, C), F32), V((CPD, 8, C), F32),
-            V((5, 8, C), F32), V((24, C), F32), V((16, C), F32), V((16, C), F32), V((C, C), F32), V((CPD, C, 128), F32), V((slots, C, C), F32),
+            V((5, 8, C), F32), V((24, C), F32), V((16, C), F32), V((16, C), F32), V((C, C), F32), V((C, 128), F32), V((slots, C, C), F32),
             V((slots, C, C), F32), V((slots, C, C), BF16), V((slots, C, C), BF16), V((slots, 16, C), F32), V((slots, 8, C), F32),
             V((ITERS, n_tgt, 8, C), F32), V((ITERS, Y_HI, 8, C), F32), V((ITERS, n_z, 8, C), F32),
             V((24, C), F32), V((Y_HI, 24, C // Y_HI), F32), V((n_z, 24, C // Y_HI), F32),

time: 64.9 us -> 64 us (0.986)
  Pallas kernels: 63.4 us -> 62.5 us
    pallas_call x1, Pallas kernels: 61.8 us -> 60.9 us  [body(): pl.pallas_call(functools.partial(kernel, n_src, n_tgt, slots, C), out_sha...]
where the time goes in v7:
time: 64 us; the launch traced here: 63.8 us
  Pallas kernels  62.5 us (98%)
  between operations  1.29 us (2%)
    pallas_call x1, Pallas kernels, body(): pl.pallas_call(functools.partial(kernel, n_src, n_tgt, slots, C), out_sha...  60.9 us
    pallas_call x1, Pallas kernels, hand_out(): pl.pallas_call(copy_kernel, out_shape=tuple((jax.ShapeDtypeStruct(a.shape...  1.58 us

profile of v7, /device:TPU:6, one launch (start us, length us, event | category | flops | bytes accessed | tf_op | source)
XLA Modules:
  0.0 63.8 jit_solution(13685876005235414326)
XLA Ops:
  1.3 60.9 %sinkhorn.1 = (f32[1,4096]{1,0:T(1,128)}, f32[1,4096]{1,0:T(1,128)}, f32[3,256]{1,0:T(4,128)}, f32[3,4096]{1,0:T(4,128)}) custom-call(f32[3,4096]{1,0:T(4,128)} %refs_0_.1, f32[3,4096]{1,0:T(4,128)} %refs_1_.1, f32[1,4096]{1,0:T(1,128)} %bitcast.5, f32[1,4096]{1,0:T(1,128)} %bitcast.6, f32[1,4096]{1,0:T(1,128)} %bitcast.7, s32[1,1,12]{2,1,0:T(1,128)} %refs_5_.1, ...), custom_call_target="tpu_custom_call" | custom-call | tf_op jit(solution)/shard_map/sinkhorn/pallas_call | solution.py:431
  62.2 1.6 %hand_out.1 = (f32[1,4096]{1,0:T(1,128)}, f32[1,4096]{1,0:T(1,128)}, f32[3,256]{1,0:T(4,128)}, f32[3,4096]{1,0:T(4,128)}) custom-call(f32[1,4096]{1,0:T(1,128)} %get-tuple-element.12.refs_0_, f32[1,4096]{1,0:T(1,128)} %get-tuple-element.13.refs_1_, f32[3,256]{1,0:T(4,128)} %get-tuple-element.14.refs_2_, f32[3,4096]{1,0:T(4,128)} %get-tuple-element.15.refs_3_), custom_call_target="tpu_custom_call" | custom-call | tf_op jit(solution)/shard_map/hand_out/pallas_call | solution.py:411

commit v8 on v7

--- a/solution.py
+++ b/solution.py
@@ -250,9 +250,9 @@
     cl[0] = jnp.log2(cl[0])
     u = over_tgt_done(0)
     kept_pass(cl[0] + u, col_scores, ts_ref)
-    over_y(0, merge(tt_ref)[0])
-    over_z(0, over_y_done(0))
-    v = -over_z_done(0)
+    over_z(0, merge(tt_ref)[0])
+    over_y(0, over_z_done(0))
+    v = -over_y_done(0)
 
     kept_pass(v - start, row_scores, tt_ref)
     over_tgt(1, merge(ts_ref)[0])

time: 64 us -> 64.4 us (level)
  no operation moved by 1% of the time
where the time goes in v8:
time: 64.4 us; the launch traced here: 63.8 us
  Pallas kernels  62.5 us (97%)
  between operations  1.29 us (2%)
    pallas_call x1, Pallas kernels, body(): pl.pallas_call(functools.partial(kernel, n_src, n_tgt, slots, C), out_sha...  60.9 us
    pallas_call x1, Pallas kernels, hand_out(): pl.pallas_call(copy_kernel, out_shape=tuple((jax.ShapeDtypeStruct(a.shape...  1.58 us

profile of v8, /device:TPU:6, one launch (start us, length us, event | category | flops | bytes accessed | tf_op | source)
XLA Modules:
  0.0 63.8 jit_solution(3677278772925905763)
XLA Ops:
  1.3 60.9 %sinkhorn.1 = (f32[1,4096]{1,0:T(1,128)}, f32[1,4096]{1,0:T(1,128)}, f32[3,256]{1,0:T(4,128)}, f32[3,4096]{1,0:T(4,128)}) custom-call(f32[3,4096]{1,0:T(4,128)} %refs_0_.1, f32[3,4096]{1,0:T(4,128)} %refs_1_.1, f32[1,4096]{1,0:T(1,128)} %bitcast.5, f32[1,4096]{1,0:T(1,128)} %bitcast.6, f32[1,4096]{1,0:T(1,128)} %bitcast.7, s32[1,1,12]{2,1,0:T(1,128)} %refs_5_.1, ...), custom_call_target="tpu_custom_call" | custom-call | tf_op jit(solution)/shard_map/sinkhorn/pallas_call | solution.py:431
  62.2 1.6 %hand_out.1 = (f32[1,4096]{1,0:T(1,128)}, f32[1,4096]{1,0:T(1,128)}, f32[3,256]{1,0:T(4,128)}, f32[3,4096]{1,0:T(4,128)}) custom-call(f32[1,4096]{1,0:T(1,128)} %get-tuple-element.12.refs_0_, f32[1,4096]{1,0:T(1,128)} %get-tuple-element.13.refs_1_, f32[3,256]{1,0:T(4,128)} %get-tuple-element.14.refs_2_, f32[3,4096]{1,0:T(4,128)} %get-tuple-element.15.refs_3_), custom_call_target="tpu_custom_call" | custom-call | tf_op jit(solution)/shard_map/hand_out/pallas_call | solution.py:411
